TPU v7x, 256 devices: a whole 4x4x8 slice. The times are simulated.
256 devices in a mesh: gx: 8 (over z), gy: 4 (over x), gz: 8 (over y, core).
Axes of the slice: x: 4, y: 4, z: 8, core: 2. Of those that a mesh axis runs over, the one named last changes fastest.
Arguments:
- fields: float32 [5, 64, 32, 1024], P(None, 'gx', 'gy', 'gz'), may hold values from -4 to 4
- tracer_ref: float32 [3, 1048576], P(None, ('gx', 'gy', 'gz')), may hold values from -1 to 1
- host_element: int32 [1048576], P(('gx', 'gy', 'gz')), may hold values from 0 to 15
- block_owner: int32 [8192, 1], P(('gx', 'gy', 'gz')), may hold values from 0 to 31; in each aligned block of 32 rows (0 to 31, 32 to 63, ...) at most 2 rows name the same one
Outputs:
- fields_out: float32 [5, 64, 32, 1024], P(None, 'gx', 'gy', 'gz')
- moved_ref: float32 [3, 1048576], P(None, ('gx', 'gy', 'gz'))
Inputs may be any that keep to these rules, and one draw needn't show every extreme that they name: `host_element`: element number of the tracer's host within the block of 1 x 1 x 16 elements of its owner, numbered (ex * 1 + ey) * 16 + ez. `block_owner`: owner of a block in its own gx slab, numbered gy * 8 + gz. Among the 32 blocks of one device at most 2 have the same owner, and some device has exactly 2 blocks with one owner.
All inputs are finite; a program needn't handle non-finite values.
Results may differ from a plain program's by a relative error of at most 0.0054.
Values sent between devices are 32-bit elements; how exact they have to be, the bound alone decides.
A program may use at most 64 MiB of HBM per device.

v0:
```python
import math

import jax
import jax.numpy as jnp
import numpy as np
from jax import lax
from jax.sharding import PartitionSpec as P

time_step = 0.01
lift_factor = 14.0
advance_factor = 0.5


def extended(block, sides, width, periodic):
    for axis, dim in sides:
        count = lax.axis_size(axis)
        forward = [(i, i + 1) for i in range(count - 1)]
        if periodic:
            forward.append((count - 1, 0))
        backward = [(target, source) for source, target in forward]
        low = lax.ppermute(
            lax.slice_in_dim(block, block.shape[dim] - width, None, axis=dim), axis, forward
        )
        high = lax.ppermute(lax.slice_in_dim(block, 0, width, axis=dim), axis, backward)
        block = jnp.concatenate([low, block, high], axis=dim)
    return block


def gll_nodes():
    return np.array(
        [
            -1.0,
            -0.8717401485096066,
            -0.5917001814331423,
            -0.2092992179024789,
            0.2092992179024789,
            0.5917001814331423,
            0.8717401485096066,
            1.0,
        ]
    )


def legendre_seven(value):
    lower = 1.0
    upper = value
    for order in range(1, 7):
        lower, upper = (upper, ((2 * order + 1) * value * upper - order * lower) / (order + 1))
    return upper


def derivative_matrix():
    points = gll_nodes()
    legendre_at = [legendre_seven(float(points[i])) for i in range(8)]
    matrix = np.zeros((8, 8))
    for i in range(8):
        for m in range(8):
            if i != m:
                matrix[i, m] = legendre_at[i] / (legendre_at[m] * (points[i] - points[m]))
    matrix[0, 0] = -14.0
    matrix[7, 7] = 14.0
    return matrix


def lagrange_rows(coordinate):
    points = gll_nodes()
    result = []
    for i in range(8):
        denominator = 1.0
        weight = jnp.ones_like(coordinate)
        for m in range(8):
            if m != i:
                denominator = denominator * (points[i] - points[m])
                weight = weight * (coordinate - float(points[m]))
        result.append(weight * float(1.0 / denominator))
    return jnp.stack(result)


def tensor_weights(coords):
    along_x = lagrange_rows(coords[0])
    along_y = lagrange_rows(coords[1])
    along_z = lagrange_rows(coords[2])
    return (
        along_x[:, None, None, :] * along_y[None, :, None, :] * along_z[None, None, :, :]
    ).reshape(512, -1)


def derivative(state, direction):
    extent = state.shape
    matrix = jnp.asarray(derivative_matrix(), jnp.float32)
    highest = lax.Precision.HIGHEST
    if direction == 1:
        shaped = state.reshape(extent[0], extent[1] // 8, 8, extent[2] * extent[3])
        result = jnp.einsum("mi,feip->femp", matrix, shaped, precision=highest)
    elif direction == 2:
        shaped = state.reshape(extent[0], extent[1], extent[2] // 8, 8, extent[3])
        result = jnp.einsum("mi,fxeiz->fxemz", matrix, shaped, precision=highest)
    else:
        blocked = np.kron(np.eye(extent[3] // 8), derivative_matrix()).T
        result = jnp.dot(
            state.reshape(-1, extent[3]), jnp.asarray(blocked, jnp.float32), precision=highest
        )
    return result.reshape(extent)


def substep(state):
    wall_halo = extended(state, (("gx", 1), ("gy", 2)), 1, False)
    cycle_halo = extended(state, (("gz", 3),), 1, True)
    previous = [wall_halo[:, :-2, 1:-1, :], wall_halo[:, 1:-1, :-2, :], cycle_halo[:, :, :, :-2]]
    following = [wall_halo[:, 2:, 1:-1, :], wall_halo[:, 1:-1, 2:, :], cycle_halo[:, :, :, 2:]]
    accumulated = jnp.zeros_like(state)
    for d in range(3):
        gradient = derivative(state, d + 1)
        position = lax.broadcasted_iota(jnp.int32, state.shape, d + 1) % 8
        face_jump = jnp.where(position == 0, previous[d] - state, 0.0) + jnp.where(
            position == 7, state - following[d], 0.0
        )
        accumulated = accumulated + state[d][None] * (lift_factor * face_jump - gradient)
    return state + time_step * accumulated


def interpolate(element_table, received):
    leading = received.shape[:-2]
    number = math.prod(leading) * 128
    element_ids = received[..., 3, :].reshape(-1).astype(jnp.int32)
    coords = jnp.moveaxis(received[..., 0:3, :], -2, 0).reshape(3, -1)
    block_size = math.gcd(number, 512)
    elements = element_table.shape[0]
    table_rows = element_table.astype(jnp.float32).reshape(elements * 3, 512)
    element_range = jnp.arange(elements, dtype=jnp.int32)

    def block_velocity(inputs):
        indices, block_coords = inputs
        weights = tensor_weights(block_coords)
        projected = jnp.dot(table_rows, weights, precision=lax.Precision.HIGHEST).reshape(
            elements, 3, -1
        )
        select = (indices[None, :] == element_range[:, None]).astype(jnp.float32)
        return jnp.sum(projected * select[:, None, :], axis=0)

    velocity = lax.map(
        block_velocity,
        (element_ids.reshape(-1, block_size), coords.reshape(3, -1, block_size).transpose(1, 0, 2)),
    )
    velocity = velocity.transpose(1, 0, 2).reshape((3,) + tuple(leading) + (128,))
    return jnp.moveaxis(velocity, 0, -2)


def shards(fields, tracer_ref, host_element, block_owner):
    half_step = substep(fields)
    final_step = substep(half_step)
    elems_x = fields.shape[1] // 8
    elems_y = fields.shape[2] // 8
    elems_z = fields.shape[3] // 8
    element_table = (
        half_step[0:3].astype(jnp.bfloat16).reshape(3, elems_x, 8, elems_y, 8, elems_z, 8)
    )
    element_table = element_table.transpose(1, 3, 5, 0, 2, 4, 6).reshape(-1, 1536)
    radial_count = lax.axis_size("gy")
    azimuth_count = lax.axis_size("gz")
    group_size = radial_count * azimuth_count
    blocks = block_owner.shape[0]
    capacity = max(2, 2 * blocks // group_size)
    owners = block_owner[:, 0]
    onehot = (owners[:, None] == jnp.arange(group_size, dtype=jnp.int32)[None, :]).astype(jnp.int32)
    earlier = jnp.cumsum(onehot, axis=0) - onehot
    arrival = jnp.sum(earlier * onehot, axis=1)
    slot_index = owners * capacity + arrival
    payload = jnp.concatenate(
        [
            tracer_ref.reshape(3, blocks, 128).transpose(1, 0, 2),
            host_element.reshape(blocks, 1, 128).astype(jnp.float32),
        ],
        axis=1,
    )
    send_buffer = (
        jnp.zeros((group_size * capacity, 4, 128), jnp.float32).at[slot_index].set(payload)
    )
    velocity = interpolate(
        element_table,
        lax.all_to_all(
            send_buffer.reshape(group_size, capacity, 4, 128),
            ("gy", "gz"),
            split_axis=0,
            concat_axis=0,
            tiled=True,
        ),
    )
    returned = lax.all_to_all(velocity, ("gy", "gz"), split_axis=0, concat_axis=0, tiled=True)
    returned = returned.reshape(group_size * capacity, 3, 128)
    own_velocity = returned[slot_index].transpose(1, 0, 2).reshape(3, blocks * 128)
    moved_ref = tracer_ref + advance_factor * own_velocity
    return (final_step, moved_ref)


def solution(mesh):
    return jax.shard_map(
        shards,
        mesh=mesh,
        in_specs=(
            P(None, "gx", "gy", "gz"),
            P(None, ("gx", "gy", "gz")),
            P(("gx", "gy", "gz")),
            P(("gx", "gy", "gz"), None),
        ),
        out_specs=(P(None, "gx", "gy", "gz"), P(None, ("gx", "gy", "gz"))),
        check_vma=False,
    )
```

profile of v0, /device:TPU:129, one launch (start us, length us, event | category | flops | bytes accessed | tf_op | source)
XLA Modules:
  0.0 96.9 jit_solution(2087244463612705393)
XLA Ops:
  0.7 1.2 %fusion.98 = (f32[5,8,8,1]{3,2,1,0:T(8,128)S(1)}, f32[5,8,8,1]{3,2,1,0:T(8,128)S(1)}) fusion(f32[5,8,8,128]{3,2,1,0:T(8,128)} %param.12), kind=kLoop, calls=%fused_computation.273 | loop fusion | bytes 5120 | tf_op jit(solution)/shard_map/slice | solution.py:22
  1.8 1.9 %collective-permute-start.4 = (f32[5,8,8,1]{3,2,1,0:T(8,128)S(1)}, f32[5,8,8,1]{3,2,1,0:T(8,128)S(1)}, u32[]{:S(2)}, u32[]{:S(2)}) collective-permute-start(f32[5,8,8,1]{3,2,1,0:T(8,128)S(1)} %get-tuple-element.238), channel_id=1, source_target_pairs={{0,1},{1,2},{2,3},{3,4},{4,5},{5,6},{6,7},{7,0},{8,9},{9,10},{10,1... | collective-permute-start | bytes 3848 | tf_op jit(solution)/shard_map/ppermute | solution.py:21
  4.4 2.6 %collective-permute-start = (f32[5,1,8,128]{3,2,1,0:T(8,128)S(1)}, f32[5,1,8,128]{3,2,1,0:T(8,128)S(1)}, u32[]{:S(2)}, u32[]{:S(2)}) collective-permute-start(f32[5,1,8,128]{3,2,1,0:T(8,128)S(1)} %get-tuple-element.237), channel_id=1, source_target_pairs={{0,32},{32,64},{64,96},{96,128},{128,160},{160,192},{192,224},{1,3... | collective-permute-start | bytes 61448 | tf_op jit(solution)/shard_map/ppermute | solution.py:21
  7.1 3.8 %collective-permute-start.1 = (f32[5,1,8,128]{3,2,1,0:T(8,128)S(1)}, f32[5,1,8,128]{3,2,1,0:T(8,128)S(1)}, u32[]{:S(2)}, u32[]{:S(2)}) collective-permute-start(f32[5,1,8,128]{3,2,1,0:T(8,128)S(1)} %get-tuple-element.236), channel_id=1, source_target_pairs={{32,0},{64,32},{96,64},{128,96},{160,128},{192,160},{224,192},{33,... | collective-permute-start | bytes 61448 | tf_op jit(solution)/shard_map/ppermute | solution.py:24
  11.7 0.8 select_reduce_fusion
  14.0 0.9 pad_maximum_fusion.16
  14.9 1.5 %scatter_fusion = f32[64,4,128]{2,1,0:T(4,128)S(1)} fusion(f32[64,4,128]{2,1,0:T(4,128)S(1)} %broadcast_in_dim.40, s32[32]{0:T(128)S(1)} %fusion.93, f32[32,4,128]{2,1,0:T(4,128)S(1)} %pad_maximum_fusion.16), kind=kCustom, calls=%fused_computation.1 | custom fusion | bytes 196736 | tf_op jit(solution)/shard_map/scatter | solution.py:177
  17.1 8.2 %all-to-all-start = ((f32[32,2,4,128]{3,1,2,0:T(2,128)}), f32[32,2,4,128]{3,1,2,0:T(2,128)S(1)}, u32[]{:S(2)}, u32[]{:S(2)}) async-start(f32[32,2,4,128]{3,1,2,0:T(2,128)} %copy.23), calls=%async_computation | async-start | bytes 262144 | tf_op jit(solution)/shard_map/all_to_all | solution.py:181
  25.9 3.3 %collective-permute-start.2 = (f32[5,10,1,128]{3,2,1,0:T(1,128)S(1)}, f32[5,10,1,128]{3,2,1,0:T(1,128)S(1)}, u32[]{:S(2)}, u32[]{:S(2)}) collective-permute-start(f32[5,10,1,128]{3,2,1,0:T(1,128)S(1)} %get-tuple-element.224), channel_id=1, source_target_pairs={{0,8},{8,16},{16,24},{1,9},{9,17},{17,25},{2,10},{10,18},{18,26},{... | collective-permute-start | bytes 76808 | tf_op jit(solution)/shard_map/ppermute | solution.py:21
  29.2 1.3 %collective-permute-start.3 = (f32[5,10,1,128]{3,2,1,0:T(1,128)S(1)}, f32[5,10,1,128]{3,2,1,0:T(1,128)S(1)}, u32[]{:S(2)}, u32[]{:S(2)}) collective-permute-start(f32[5,10,1,128]{3,2,1,0:T(1,128)S(1)} %get-tuple-element.225), channel_id=1, source_target_pairs={{8,0},{16,8},{24,16},{9,1},{17,9},{25,17},{10,2},{18,10},{26,18},{... | collective-permute-start | bytes 76808 | tf_op jit(solution)/shard_map/ppermute | solution.py:24
  30.8 2.9 %collective-permute-done.3 = f32[5,10,1,128]{3,2,1,0:T(1,128)S(1)} collective-permute-done((f32[5,10,1,128]{3,2,1,0:T(1,128)S(1)}, f32[5,10,1,128]{3,2,1,0:T(1,128)S(1)}, u32[]{:S(2)}, u32[]{:S(2)}) %collective-permute-start.3) | collective-permute-done | bytes 25632 | tf_op jit(solution)/shard_map/ppermute | solution.py:24
  34.8 0.8 fusion.96
  35.7 1.9 %collective-permute-start.6 = (f32[5,1,8,128]{3,2,1,0:T(8,128)}, f32[5,1,8,128]{3,2,1,0:T(8,128)}, u32[]{:S(2)}, u32[]{:S(2)}) collective-permute-start(f32[5,1,8,128]{3,2,1,0:T(8,128)} %get-tuple-element.229), channel_id=1, source_target_pairs={{0,32},{32,64},{64,96},{96,128},{128,160},{160,192},{192,224},{1,3... | collective-permute-start | bytes 61448 | tf_op jit(solution)/shard_map/ppermute | solution.py:21
  37.6 4.6 %collective-permute-start.7 = (f32[5,1,8,128]{3,2,1,0:T(8,128)}, f32[5,1,8,128]{3,2,1,0:T(8,128)}, u32[]{:S(2)}, u32[]{:S(2)}) collective-permute-start(f32[5,1,8,128]{3,2,1,0:T(8,128)} %get-tuple-element.230), channel_id=1, source_target_pairs={{32,0},{64,32},{96,64},{128,96},{160,128},{192,160},{224,192},{33,... | collective-permute-start | bytes 61448 | tf_op jit(solution)/shard_map/ppermute | solution.py:24
  42.2 3.4 %collective-permute-start.10 = (f32[5,8,8,1]{3,2,1,0:T(8,128)}, f32[5,8,8,1]{3,2,1,0:T(8,128)}, u32[]{:S(2)}, u32[]{:S(2)}) collective-permute-start(f32[5,8,8,1]{3,2,1,0:T(8,128)} %get-tuple-element.231), channel_id=1, source_target_pairs={{0,1},{1,2},{2,3},{3,4},{4,5},{5,6},{6,7},{7,0},{8,9},{9,10},{10,1... | collective-permute-start | bytes 3848 | tf_op jit(solution)/shard_map/ppermute | solution.py:21
  45.6 0.9 convolution_bitcast_fusion.2
  46.5 0.8 reshape.1776
  48.0 0.8 reshape.1775
  48.8 1.9 %collective-permute-done.11 = f32[5,8,8,1]{3,2,1,0:T(8,128)} collective-permute-done((f32[5,8,8,1]{3,2,1,0:T(8,128)}, f32[5,8,8,1]{3,2,1,0:T(8,128)}, u32[]{:S(2)}, u32[]{:S(2)}) %collective-permute-start.11) | collective-permute-done | bytes 1312 | tf_op jit(solution)/shard_map/ppermute | solution.py:24
  50.7 1.3 %fusion.50 = f32[5,8,8,128]{3,2,1,0:T(8,128)S(1)} fusion(f32[5,8,8,128]{3,2,1,0:T(8,128)S(1)} %fusion.42, f32[128,128,1,1]{1,0,3,2:T(8,128)S(1)} %copy-done.6, f32[5,8,8,1]{3,2,1,0:T(8,128)} %collective-permute-done.11, f32[5,8,8,1]{3,2,1,0:T(8,128)} %collective-permute-done.10, f32[8,8,128]{2,1,0:T(8,128)S(1)} %get-tuple-element.228, ...), kind=kOutput, calls=%fused_computation.175 | convolution fusion | flops 63447040 | bytes 429696 | tf_op jit(solution)/shard_map/dot_general | solution.py:100
  52.0 0.8 pad_maximum_fusion.19
  52.8 3.1 %collective-permute-start.8 = (f32[5,10,1,128]{3,2,1,0:T(1,128)S(1)}, f32[5,10,1,128]{3,2,1,0:T(1,128)S(1)}, u32[]{:S(2)}, u32[]{:S(2)}) collective-permute-start(f32[5,10,1,128]{3,2,1,0:T(1,128)S(1)} %get-tuple-element.222), channel_id=1, source_target_pairs={{0,8},{8,16},{16,24},{1,9},{9,17},{17,25},{2,10},{10,18},{18,26},{... | collective-permute-start | bytes 76808 | tf_op jit(solution)/shard_map/ppermute | solution.py:21
  55.9 1.3 %collective-permute-start.9 = (f32[5,10,1,128]{3,2,1,0:T(1,128)S(1)}, f32[5,10,1,128]{3,2,1,0:T(1,128)S(1)}, u32[]{:S(2)}, u32[]{:S(2)}) collective-permute-start(f32[5,10,1,128]{3,2,1,0:T(1,128)S(1)} %get-tuple-element.223), channel_id=1, source_target_pairs={{8,0},{16,8},{24,16},{9,1},{17,9},{25,17},{10,2},{18,10},{26,18},{... | collective-permute-start | bytes 76808 | tf_op jit(solution)/shard_map/ppermute | solution.py:24
  57.5 22.3 %while.14 = (s32[]{:T(128)}, f32[16,3,512]{2,1,0:T(4,128)S(1)}, f32[16,3,512]{2,0,1:T(8,128)S(1)}, f32[48,512]{1,0:T(8,128)S(1)}, s32[16,512]{1,0:T(8,128)S(1)}, /*index=5*/s32[]{:T(128)}, s32[]{:T(128)}, s32[]{}, s32[]{}) while((s32[]{:T(128)}, f32[16,3,512]{2,1,0:T(4,128)S(1)}, f32[16,3,512]{2,0,1:T(8,128)S(1)}, ...), condition=%wide.region_5.6_spmd.clone, body=%wide.region_3.5_spmd.clone.sunk | while | flops 151446016 | bytes 3170445 | solution.py:141
  63.5 0.8 convolution_bitcast_fusion.7
  64.9 0.8 convolution_bitcast_fusion.7
  69.1 0.8 convolution_bitcast_fusion.7
  70.5 0.8 convolution_bitcast_fusion.7
  76.1 0.8 convolution_bitcast_fusion.7
  80.6 7.6 %all-to-all-start.1 = ((f32[32,2,3,128]{3,1,2,0:T(2,128)}), f32[32,2,3,128]{3,1,2,0:T(2,128)S(1)}, u32[]{:S(2)}, u32[]{:S(2)}) async-start(f32[32,2,3,128]{3,1,2,0:T(2,128)} %copy.28), calls=%async_computation.1 | async-start | bytes 196608 | tf_op jit(solution)/shard_map/all_to_all | solution.py:189
  88.2 1.8 %fusion.49 = f32[5,8,8,128]{3,2,1,0:T(8,128)} fusion(f32[5,8,8,128]{3,2,1,0:T(8,128)S(1)} %fusion.42, f32[5,8,8,128]{3,2,1,0:T(8,128)S(1)} %fusion.50, f32[8,8,1,1]{1,0,3,2:T(8,128)S(1)} %copy-done.7, f32[5,8,8,128]{3,1,2,0:T(8,128)S(1)} %copy-done.2, f32[5,10,1,128]{3,2,1,0:T(1,128)S(1)} %collective-permute-done.9, ...), kind=kOutput, calls=%fused_computation.173 | convolution fusion | flops 5324800 | bytes 813384 | tf_op jit(solution)/shard_map/mi,fxeiz->fxemz/dot_general | solution.py:97
  90.0 5.6 %all-to-all-done.1 = f32[32,2,3,128]{3,1,2,0:T(2,128)S(1)} async-done(((f32[32,2,3,128]{3,1,2,0:T(2,128)}), f32[32,2,3,128]{3,1,2,0:T(2,128)S(1)}, u32[]{:S(2)}, u32[]{:S(2)}) %all-to-all-start.1) | async-done | bytes 98336 | tf_op jit(solution)/shard_map/all_to_all | solution.py:189
  (302 shorter events, 25.3 us)
Async XLA Ops:
  0.6 24.8 %copy-start.4 = (f32[8,8,1]{1,0,2:T(8,128)S(1)}, f32[8,8,1]{1,0,2:T(8,128)}, u32[]{:S(2)}) copy-start(f32[8,8,1]{1,0,2:T(8,128)} %constant.196) | copy-start | bytes 772
  0.6 29.8 %copy-start.5 = (f32[128,128,1,1]{1,0,3,2:T(8,128)S(1)}, f32[128,128,1,1]{1,0,3,2:T(8,128)}, u32[]{:S(2)}) copy-start(f32[128,128,1,1]{1,0,3,2:T(8,128)} %constant.198) | copy-start | bytes 196612
  0.7 24.6 %copy-start = (f32[5,8,8,128]{3,2,1,0:T(8,128)S(1)}, f32[5,8,8,128]{3,2,1,0:T(8,128)}, u32[]{:S(2)}) copy-start(f32[5,8,8,128]{3,2,1,0:T(8,128)} %param.12) | copy-start | bytes 491524
  1.8 28.6 %collective-permute-start.4 = (f32[5,8,8,1]{3,2,1,0:T(8,128)S(1)}, f32[5,8,8,1]{3,2,1,0:T(8,128)S(1)}, u32[]{:S(2)}, u32[]{:S(2)}) collective-permute-start(f32[5,8,8,1]{3,2,1,0:T(8,128)S(1)} %get-tuple-element.238), channel_id=1, source_target_pairs={{0,1},{1,2},{2,3},{3,4},{4,5},{5,6},{6,7},{7,0},{8,9},{9,10},{10,1... | collective-permute-start | bytes 3848 | tf_op jit(solution)/shard_map/ppermute | solution.py:21
  3.7 26.8 %collective-permute-start.5 = (f32[5,8,8,1]{3,2,1,0:T(8,128)S(1)}, f32[5,8,8,1]{3,2,1,0:T(8,128)S(1)}, u32[]{:S(2)}, u32[]{:S(2)}) collective-permute-start(f32[5,8,8,1]{3,2,1,0:T(8,128)S(1)} %get-tuple-element.239), channel_id=1, source_target_pairs={{1,0},{2,1},{3,2},{4,3},{5,4},{6,5},{7,6},{0,7},{9,8},{10,9},{11,1... | collective-permute-start | bytes 3848 | tf_op jit(solution)/shard_map/ppermute | solution.py:24
  4.4 21.3 %collective-permute-start = (f32[5,1,8,128]{3,2,1,0:T(8,128)S(1)}, f32[5,1,8,128]{3,2,1,0:T(8,128)S(1)}, u32[]{:S(2)}, u32[]{:S(2)}) collective-permute-start(f32[5,1,8,128]{3,2,1,0:T(8,128)S(1)} %get-tuple-element.237), channel_id=1, source_target_pairs={{0,32},{32,64},{64,96},{96,128},{128,160},{160,192},{192,224},{1,3... | collective-permute-start | bytes 61448 | tf_op jit(solution)/shard_map/ppermute | solution.py:21
  7.1 18.7 %collective-permute-start.1 = (f32[5,1,8,128]{3,2,1,0:T(8,128)S(1)}, f32[5,1,8,128]{3,2,1,0:T(8,128)S(1)}, u32[]{:S(2)}, u32[]{:S(2)}) collective-permute-start(f32[5,1,8,128]{3,2,1,0:T(8,128)S(1)} %get-tuple-element.236), channel_id=1, source_target_pairs={{32,0},{64,32},{96,64},{128,96},{160,128},{192,160},{224,192},{33,... | collective-permute-start | bytes 61448 | tf_op jit(solution)/shard_map/ppermute | solution.py:24
  14.0 19.8 %copy-start.7 = (f32[8,8,1,1]{1,0,3,2:T(8,128)S(1)}, f32[8,8,1,1]{1,0,3,2:T(8,128)}, u32[]{:S(2)}) copy-start(f32[8,8,1,1]{1,0,3,2:T(8,128)} %constant.197) | copy-start | bytes 772
  17.1 40.2 %all-to-all-start = ((f32[32,2,4,128]{3,1,2,0:T(2,128)}), f32[32,2,4,128]{3,1,2,0:T(2,128)S(1)}, u32[]{:S(2)}, u32[]{:S(2)}) async-start(f32[32,2,4,128]{3,1,2,0:T(2,128)} %copy.23), calls=%async_computation | async-start | bytes 262144 | tf_op jit(solution)/shard_map/all_to_all | solution.py:181
  25.3 8.8 %copy-start.8 = (s32[128]{0:T(128)}, s32[128]{0:T(128)S(1)}, u32[]{:S(2)}) copy-start(s32[128]{0:T(128)S(1)} %get-tuple-element.240) | copy-start | bytes 1540
  25.3 8.8 %copy-start.10 = (s32[128]{0:T(128)}, s32[128]{0:T(128)S(1)}, u32[]{:S(2)}) copy-start(s32[128]{0:T(128)S(1)} %get-tuple-element.241) | copy-start | bytes 1540
  25.4 8.8 %copy-start.14 = (pred[128]{0:T(512)(128)(4,1)}, pred[128]{0:T(512)(128)(4,1)S(1)}, u32[]{:S(2)}) copy-start(pred[128]{0:T(512)(128)(4,1)S(1)} %compare_and_fusion) | copy-start | bytes 388
  25.7 8.5 %copy-start.12 = (pred[8]{0:T(512)(128)(4,1)}, pred[8]{0:T(512)(128)(4,1)S(1)}, u32[]{:S(2)}) copy-start(pred[8]{0:T(512)(128)(4,1)S(1)} %compare_and_fusion.1) | copy-start | bytes 28
  25.9 4.9 %collective-permute-start.2 = (f32[5,10,1,128]{3,2,1,0:T(1,128)S(1)}, f32[5,10,1,128]{3,2,1,0:T(1,128)S(1)}, u32[]{:S(2)}, u32[]{:S(2)}) collective-permute-start(f32[5,10,1,128]{3,2,1,0:T(1,128)S(1)} %get-tuple-element.224), channel_id=1, source_target_pairs={{0,8},{8,16},{16,24},{1,9},{9,17},{17,25},{2,10},{10,18},{18,26},{... | collective-permute-start | bytes 76808 | tf_op jit(solution)/shard_map/ppermute | solution.py:21
  29.2 4.6 %collective-permute-start.3 = (f32[5,10,1,128]{3,2,1,0:T(1,128)S(1)}, f32[5,10,1,128]{3,2,1,0:T(1,128)S(1)}, u32[]{:S(2)}, u32[]{:S(2)}) collective-permute-start(f32[5,10,1,128]{3,2,1,0:T(1,128)S(1)} %get-tuple-element.225), channel_id=1, source_target_pairs={{8,0},{16,8},{24,16},{9,1},{17,9},{25,17},{10,2},{18,10},{26,18},{... | collective-permute-start | bytes 76808 | tf_op jit(solution)/shard_map/ppermute | solution.py:24
  35.7 16.3 %collective-permute-start.6 = (f32[5,1,8,128]{3,2,1,0:T(8,128)}, f32[5,1,8,128]{3,2,1,0:T(8,128)}, u32[]{:S(2)}, u32[]{:S(2)}) collective-permute-start(f32[5,1,8,128]{3,2,1,0:T(8,128)} %get-tuple-element.229), channel_id=1, source_target_pairs={{0,32},{32,64},{64,96},{96,128},{128,160},{160,192},{192,224},{1,3... | collective-permute-start | bytes 61448 | tf_op jit(solution)/shard_map/ppermute | solution.py:21
  37.6 14.4 %collective-permute-start.7 = (f32[5,1,8,128]{3,2,1,0:T(8,128)}, f32[5,1,8,128]{3,2,1,0:T(8,128)}, u32[]{:S(2)}, u32[]{:S(2)}) collective-permute-start(f32[5,1,8,128]{3,2,1,0:T(8,128)} %get-tuple-element.230), channel_id=1, source_target_pairs={{32,0},{64,32},{96,64},{128,96},{160,128},{192,160},{224,192},{33,... | collective-permute-start | bytes 61448 | tf_op jit(solution)/shard_map/ppermute | solution.py:24
  42.2 6.6 %collective-permute-start.10 = (f32[5,8,8,1]{3,2,1,0:T(8,128)}, f32[5,8,8,1]{3,2,1,0:T(8,128)}, u32[]{:S(2)}, u32[]{:S(2)}) collective-permute-start(f32[5,8,8,1]{3,2,1,0:T(8,128)} %get-tuple-element.231), channel_id=1, source_target_pairs={{0,1},{1,2},{2,3},{3,4},{4,5},{5,6},{6,7},{7,0},{8,9},{9,10},{10,1... | collective-permute-start | bytes 3848 | tf_op jit(solution)/shard_map/ppermute | solution.py:21
  45.6 5.1 %collective-permute-start.11 = (f32[5,8,8,1]{3,2,1,0:T(8,128)}, f32[5,8,8,1]{3,2,1,0:T(8,128)}, u32[]{:S(2)}, u32[]{:S(2)}) collective-permute-start(f32[5,8,8,1]{3,2,1,0:T(8,128)} %get-tuple-element.232), channel_id=1, source_target_pairs={{1,0},{2,1},{3,2},{4,3},{5,4},{6,5},{7,6},{0,7},{9,8},{10,9},{11,1... | collective-permute-start | bytes 3848 | tf_op jit(solution)/shard_map/ppermute | solution.py:24
  47.9 2.8 %copy-start.6 = (f32[128,128,1,1]{1,0,3,2:T(8,128)S(1)}, f32[128,128,1,1]{1,0,3,2:T(8,128)}, u32[]{:S(2)}) copy-start(f32[128,128,1,1]{1,0,3,2:T(8,128)} %constant.198) | copy-start | bytes 196612
  47.9 2.7 %copy-start.9 = (s32[128]{0:T(128)S(1)}, s32[128]{0:T(128)}, u32[]{:S(2)}) copy-start(s32[128]{0:T(128)} %copy-done.8) | copy-start | bytes 1540
  47.9 2.7 %copy-start.11 = (s32[128]{0:T(128)S(1)}, s32[128]{0:T(128)}, u32[]{:S(2)}) copy-start(s32[128]{0:T(128)} %copy-done.10) | copy-start | bytes 1540
  47.9 2.7 %copy-start.15 = (pred[128]{0:T(512)(128)(4,1)S(1)}, pred[128]{0:T(512)(128)(4,1)}, u32[]{:S(2)}) copy-start(pred[128]{0:T(512)(128)(4,1)} %copy-done.14) | copy-start | bytes 388
  48.0 9.5 %copy-start.3 = (f32[16,3,512]{2,1,0:T(4,128)S(1)}, f32[16,3,512]{2,1,0:T(4,128)}, u32[]{:S(2)}) copy-start(f32[16,3,512]{2,1,0:T(4,128)} %custom-call.3) | copy-start | bytes 294916
  52.8 35.3 %collective-permute-start.8 = (f32[5,10,1,128]{3,2,1,0:T(1,128)S(1)}, f32[5,10,1,128]{3,2,1,0:T(1,128)S(1)}, u32[]{:S(2)}, u32[]{:S(2)}) collective-permute-start(f32[5,10,1,128]{3,2,1,0:T(1,128)S(1)} %get-tuple-element.222), channel_id=1, source_target_pairs={{0,8},{8,16},{16,24},{1,9},{9,17},{17,25},{2,10},{10,18},{18,26},{... | collective-permute-start | bytes 76808 | tf_op jit(solution)/shard_map/ppermute | solution.py:21
  55.9 32.2 %collective-permute-start.9 = (f32[5,10,1,128]{3,2,1,0:T(1,128)S(1)}, f32[5,10,1,128]{3,2,1,0:T(1,128)S(1)}, u32[]{:S(2)}, u32[]{:S(2)}) collective-permute-start(f32[5,10,1,128]{3,2,1,0:T(1,128)S(1)} %get-tuple-element.223), channel_id=1, source_target_pairs={{8,0},{16,8},{24,16},{9,1},{17,9},{25,17},{10,2},{18,10},{26,18},{... | collective-permute-start | bytes 76808 | tf_op jit(solution)/shard_map/ppermute | solution.py:24
  57.5 30.7 %copy-start.2 = (f32[5,8,8,128]{3,1,2,0:T(8,128)S(1)}, f32[5,8,8,128]{3,1,2,0:T(8,128)}, u32[]{:S(2)}) copy-start(f32[5,8,8,128]{3,1,2,0:T(8,128)} %convolution_bitcast_fusion.2) | copy-start | bytes 491524
  57.5 30.7 %copy-start.13 = (pred[8]{0:T(512)(128)(4,1)S(1)}, pred[8]{0:T(512)(128)(4,1)}, u32[]{:S(2)}) copy-start(pred[8]{0:T(512)(128)(4,1)} %copy-done.12) | copy-start | bytes 28
  79.8 16.4 %copy-start.1 = (f32[3,4096]{1,0:T(4,128)S(1)}, f32[3,4096]{1,0:T(4,128)}, u32[]{:S(2)}) copy-start(f32[3,4096]{1,0:T(4,128)} %param.13) | copy-start | bytes 147460
  80.6 15.0 %all-to-all-start.1 = ((f32[32,2,3,128]{3,1,2,0:T(2,128)}), f32[32,2,3,128]{3,1,2,0:T(2,128)S(1)}, u32[]{:S(2)}, u32[]{:S(2)}) async-start(f32[32,2,3,128]{3,1,2,0:T(2,128)} %copy.28), calls=%async_computation.1 | async-start | bytes 196608 | tf_op jit(solution)/shard_map/all_to_all | solution.py:189
where the time goes:
time: 97.7 us; the launch traced here: 96.9 us
  starting transfers between devices  43 us (44%)
  matrix products  17.3 us (18%)
  local copies, waits for them, and re-layouts  12.5 us (13%)
  other arithmetic  11 us (11%)
  waiting for transfers between devices  10.4 us (11%)
  loops' own time  1.43 us (1%)
  between operations  1.26 us (1%)
    ppermute x6, starting transfers between devices, extended(): lax.ppermute(lax.slice_in_dim(block, block.shape[dim] - width, None, axis...  16.2 us
    dot_general x16, matrix products, block_velocity(): jnp.dot(table_rows, weights, precision=lax.Precision.HIGHEST)  12.3 us
    ppermute x6, starting transfers between devices, extended(): lax.ppermute(lax.slice_in_dim(block, 0, width, axis=dim), axis, backward)  11 us
    all_to_all x1, starting transfers between devices, shards(): lax.all_to_all(send_buffer.reshape(group_size, capacity, 4, 128), ('gy',...  8.21 us
    all_to_all x1, starting transfers between devices, shards(): lax.all_to_all(velocity, ('gy', 'gz'), split_axis=0, concat_axis=0, tiled...  7.58 us
    all_to_all x1, waiting for transfers between devices, shards(): lax.all_to_all(velocity, ('gy', 'gz'), split_axis=0, concat_axis=0, tiled...  5.58 us
    ppermute x6, waiting for transfers between devices, extended(): lax.ppermute(lax.slice_in_dim(block, 0, width, axis=dim), axis, backward)  4.83 us
    slice x4, local copies, waits for them, and re-layouts, extended(): lax.slice_in_dim(block, block.shape[dim] - width, None, axis=dim)  2.58 us
  transfers between devices with their start and end apart: 14, of which 3 were waited for; matrix products, arithmetic and copies ran while one was open for 39% of the time, Pallas kernels for 0%

commit v1 on v0

v1 whole, which is shorter than its diff:
```python
import functools

import jax
import jax.numpy as jnp
import numpy as np
from jax import lax
from jax.experimental import pallas as pl
from jax.experimental.pallas import tpu as pltpu
from jax.sharding import PartitionSpec as P

TIME_STEP = 0.01
LIFT = 14.0
ADVANCE = 0.5
F32 = jnp.float32
BF16 = jnp.bfloat16
MESH = pl.DeviceIdType.MESH


def gll_nodes():
    return np.array(
        [
            -1.0,
            -0.8717401485096066,
            -0.5917001814331423,
            -0.2092992179024789,
            0.2092992179024789,
            0.5917001814331423,
            0.8717401485096066,
            1.0,
        ]
    )


def legendre_seven(value):
    lower = 1.0
    upper = value
    for order in range(1, 7):
        lower, upper = (upper, ((2 * order + 1) * value * upper - order * lower) / (order + 1))
    return upper


def derivative_matrix():
    points = gll_nodes()
    legendre_at = [legendre_seven(float(points[i])) for i in range(8)]
    matrix = np.zeros((8, 8))
    for i in range(8):
        for m in range(8):
            if i != m:
                matrix[i, m] = legendre_at[i] / (legendre_at[m] * (points[i] - points[m]))
    matrix[0, 0] = -14.0
    matrix[7, 7] = 14.0
    return matrix


def split(matrix):
    high = np.asarray(matrix, np.float32).astype(BF16)
    low = (np.asarray(matrix, np.float64) - high.astype(np.float64)).astype(np.float32).astype(BF16)
    return high, low


def constants():
    element = -derivative_matrix()
    element[0, 0] -= LIFT
    element[7, 7] += LIFT
    element = element * TIME_STEP
    eye = np.eye(8)
    both = np.concatenate([np.kron(element, eye), np.kron(eye, element)], 0)
    high, low = split(both)
    planes = np.concatenate([high, high, low], 1)
    line = np.kron(np.eye(16), element)
    for e in range(1, 16):
        line[8 * e, 8 * e - 1] = LIFT * TIME_STEP
        line[8 * e - 1, 8 * e] = -LIFT * TIME_STEP
    high, low = split(line.T)
    line = np.concatenate(
        [
            np.concatenate([high, low], 1),
            np.concatenate([high, np.zeros_like(low)], 1),
        ],
        0,
    )
    points = gll_nodes()
    rows = np.zeros((8, 8))
    for n in range(8):
        others = [points[m] for m in range(8) if m != n]
        rows[:7, n] = others
        rows[7, n] = 1.0 / np.prod([points[n] - other for other in others])
    nodes = np.broadcast_to(rows[:, :, None], (8, 8, 128)).astype(np.float32)
    return planes, line, nodes


def halves(value):
    high = value.astype(BF16)
    low = (value - high.astype(F32)).astype(BF16)
    return high, low


def dot(a, b):
    return jnp.dot(a, b, preferred_element_type=F32)


def body(
    sizes,
    fields_hbm,
    tracer_hbm,
    host_hbm,
    owner_hbm,
    planes_hbm,
    line_hbm,
    nodes_hbm,
    final_hbm,
    moved_hbm,
    state,
    half,
    part,
    final,
    tracer,
    host,
    owner,
    planes,
    line,
    nodes,
    y_out,
    z_out,
    x_in,
    y_in,
    z_in,
    payload,
    unpack,
    outgoing,
    received,
    z_weights,
    xy_weights,
    velocity,
    returned,
    own_velocity,
    moved,
    load_sem,
    halo_send,
    halo_recv,
    route_send,
    route_recv,
    own_sem,
    store_sem,
):
    n_gx, n_gy, n_gz, blocks = sizes
    group = n_gy * n_gz
    gx, gy, gz = lax.axis_index("gx"), lax.axis_index("gy"), lax.axis_index("gz")
    me = gy * n_gz + gz

    loads = [
        pltpu.make_async_copy(source, target, load_sem.at[i])
        for i, (source, target) in enumerate(
            [
                (fields_hbm, state),
                (owner_hbm, owner),
                (tracer_hbm, tracer),
                (host_hbm, host),
                (planes_hbm, planes),
                (line_hbm, line),
                (nodes_hbm, nodes),
            ]
        )
    ]
    for load in loads:
        load.start()

    def peer(k):
        to_y = lax.rem(gy + k // n_gz, n_gy)
        to_z = lax.rem(gz + lax.rem(k, n_gz), n_gz)
        return to_y, to_z

    barrier = pltpu.get_barrier_semaphore()

    def greet(k, carry):
        to_y, to_z = peer(k)
        pl.semaphore_signal(barrier, inc=1, device_id=(gx, to_y, to_z), device_id_type=MESH)
        return carry

    x_low, x_high = lax.rem(gx + n_gx - 1, n_gx), lax.rem(gx + 1, n_gx)
    y_low, y_high = lax.rem(gy + n_gy - 1, n_gy), lax.rem(gy + 1, n_gy)
    z_low, z_high = lax.rem(gz + n_gz - 1, n_gz), lax.rem(gz + 1, n_gz)
    for x in (x_low, x_high):
        pl.semaphore_signal(barrier, inc=1, device_id=(x, gy, gz), device_id_type=MESH)
    lax.fori_loop(1, group, greet, 0)

    lane = lax.broadcasted_iota(jnp.int32, (8, 128), 1)
    sub = lax.broadcasted_iota(jnp.int32, (8, 128), 0)

    def fill_halos(source, step):
        for f in range(5):
            y_out[step, 0, f] = source[f, :, 0, :]
            y_out[step, 1, f] = source[f, :, 7, :]
        packed = jnp.zeros((8, 128), F32)
        for f in range(5):
            for x in range(8):
                at = f * 8 + x
                packed = jnp.where(
                    lane // 2 == at, pltpu.roll(source[f, x], (1 + 2 * at) % 128, 1), packed
                )
        z_out[step] = packed

    def halo_copies(source, step):
        sides = [
            (source.at[:, 0], x_in.at[step, 1], (x_low, gy, gz)),
            (source.at[:, 7], x_in.at[step, 0], (x_high, gy, gz)),
            (y_out.at[step, 0], y_in.at[step, 1], (gx, y_low, gz)),
            (y_out.at[step, 1], y_in.at[step, 0], (gx, y_high, gz)),
            (z_out.at[step], z_in.at[step, 1], (gx, gy, z_low)),
            (z_out.at[step], z_in.at[step, 0], (gx, gy, z_high)),
        ]
        return [
            pltpu.make_async_remote_copy(
                src_ref=source_ref,
                dst_ref=target_ref,
                send_sem=halo_send.at[step, i],
                recv_sem=halo_recv.at[step, i],
                device_id=device,
                device_id_type=MESH,
            )
            for i, (source_ref, target_ref, device) in enumerate(sides)
        ]

    def inner(source):
        wind = [source[d].reshape(64, 128) for d in range(3)]
        for f in range(5):
            value = source[f].reshape(64, 128)
            high, low = halves(value)
            across = dot(planes[...], jnp.concatenate([high, low, high], 0))
            along = dot(jnp.concatenate([high, low], 1), line[...])
            total = value + wind[0] * across[:64] + wind[1] * across[64:]
            total = total + wind[2] * (along[:, :128] + along[:, 128:])
            part[f] = total.reshape(8, 8, 128)

    lift = LIFT * TIME_STEP
    x_prev = jnp.where(gx == 0, 0.0, lift)
    x_next = jnp.where(gx == n_gx - 1, 0.0, -lift)
    y_prev = jnp.where(sub == 0, jnp.where(gy == 0, 0.0, lift), 0.0)
    y_next = jnp.where(sub == 7, jnp.where(gy == n_gy - 1, 0.0, -lift), 0.0)
    z_side = jnp.where(lane == 0, lift, 0.0) + jnp.where(lane == 127, -lift, 0.0)

    def outer(source, target, step):
        merged = jnp.where(
            lane % 2 == 0,
            pltpu.roll(z_in[step, 1], 127, 1),
            pltpu.roll(z_in[step, 0], 1, 1),
        )
        for x in range(8):
            wind = [source[d, x] for d in range(3)]
            y_wind = (wind[1] * y_prev, wind[1] * y_next)
            z_wind = wind[2] * z_side
            for f in range(5):
                at = f * 8 + x
                total = part[f, x]
                if x == 0:
                    total = total + wind[0] * (x_prev * x_in[step, 0, f])
                if x == 7:
                    total = total + wind[0] * (x_next * x_in[step, 1, f])
                total = total + y_wind[0] * y_in[step, 0, f, pl.ds(x, 1), :]
                total = total + y_wind[1] * y_in[step, 1, f, pl.ds(x, 1), :]
                total = total + z_wind * pltpu.roll(merged, (127 - 2 * at) % 128, 1)
                target[f, x] = total

    for load in loads[1:4]:
        load.wait()
    owner_column = jnp.broadcast_to(owner[...].astype(F32), (blocks, 128))
    row = lax.broadcasted_iota(jnp.int32, (blocks, 128), 0)
    column = lax.broadcasted_iota(jnp.int32, (blocks, 128), 1)
    block_lane = lax.rem(column, blocks)
    owner_lane = jnp.sum(jnp.where(row == block_lane, owner_column, 0.0), axis=0, keepdims=True)
    same = owner_column == owner_lane
    earlier_lane = jnp.sum(
        jnp.where(same & (row < block_lane), 1.0, 0.0), axis=0, keepdims=True
    )
    earlier_column = jnp.sum(
        jnp.where(same & (column < row), 1.0, 0.0), axis=1, keepdims=True
    )
    slot_lane = owner_lane * 8.0 + earlier_lane * 4.0
    slot_column = owner_column[:, :1] * 8.0 + earlier_column * 4.0
    for c in range(3):
        wide = lax.broadcasted_iota(jnp.int32, (blocks, group * 8), 1).astype(F32)
        unpack[c * blocks : (c + 1) * blocks, :] = jnp.where(
            wide == slot_column + float(c), 1.0, 0.0
        ).astype(BF16)
    for b in range(blocks):
        payload[pl.ds(b, 3, stride=blocks), :] = tracer[:, b * 128 : (b + 1) * 128]
    payload[3 * blocks :, :] = host[...].astype(F32)
    width = 4 * blocks
    tall = lax.broadcasted_iota(jnp.int32, (group * 8, width), 0).astype(F32)
    part_lane = lax.broadcasted_iota(jnp.int32, (1, width), 1) // blocks
    target_row = slot_lane[:, :width] + part_lane.astype(F32)
    place = jnp.where(tall == target_row, 1.0, 0.0).astype(BF16)
    high, low = halves(payload[...])
    packed = dot(
        jnp.concatenate([place, place], 1), jnp.concatenate([high, low], 0)
    )
    outgoing[...] = packed.reshape(group, 8, 128)

    loads[0].wait()
    fill_halos(state, 0)

    pl.semaphore_wait(barrier, group + 1)

    first = halo_copies(state, 0)
    for copy in first:
        copy.start()

    def send_block(k, carry):
        to_y, to_z = peer(k)
        pltpu.make_async_remote_copy(
            src_ref=outgoing.at[to_y * n_gz + to_z],
            dst_ref=received.at[me],
            send_sem=route_send.at[0],
            recv_sem=route_recv.at[0],
            device_id=(gx, to_y, to_z),
            device_id_type=MESH,
        ).start()
        return carry

    lax.fori_loop(1, group, send_block, 0)
    mine = pltpu.make_async_copy(outgoing.at[me], received.at[me], own_sem.at[0])
    mine.start()

    loads[4].wait()
    loads[5].wait()
    inner(state)
    for copy in first:
        copy.wait_recv()
    outer(state, half, 0)
    fill_halos(half, 1)
    second = halo_copies(half, 1)
    for copy in second:
        copy.start()

    loads[6].wait()
    mine.wait()
    others = received.at[pl.ds(0, group - 1)]
    pltpu.make_async_copy(others, others, route_recv.at[0]).wait()

    def lagrange(coordinate):
        value = nodes[7]
        for k in range(7):
            value = value * (coordinate - nodes[k])
        return value

    def weigh(s, carry):
        for a in range(2):
            lanes = slice(a * 128, (a + 1) * 128)
            coordinate = [received[s, 4 * a + c : 4 * a + c + 1, :] for c in range(4)]
            along = [lagrange(coordinate[c]) for c in range(3)]
            for e in range(16):
                z_weights[s, e * 8 : (e + 1) * 8, lanes] = jnp.where(
                    coordinate[3] == float(e), along[2], 0.0
                ).astype(BF16)
            for i in range(8):
                xy_weights[s, i * 8 : (i + 1) * 8, lanes] = along[0][i : i + 1, :] * along[1]
        return carry

    lax.fori_loop(0, group, weigh, 0)

    table = half[0:3].reshape(192, 128).astype(BF16)

    def interpolate(s):
        values = dot(table, z_weights[s])
        for a in range(2):
            lanes = slice(a * 128, (a + 1) * 128)
            weights = xy_weights[s, :, lanes]
            rows = [
                jnp.sum(values[c * 64 : (c + 1) * 64, lanes] * weights, axis=0, keepdims=True)
                for c in range(3)
            ]
            velocity[s, 4 * a : 4 * a + 4, :] = jnp.concatenate(rows + [jnp.zeros_like(rows[0])], 0)

    def send_back(k, carry):
        to_y, to_z = peer(k)
        s = to_y * n_gz + to_z
        interpolate(s)
        pltpu.make_async_remote_copy(
            src_ref=velocity.at[s],
            dst_ref=returned.at[me],
            send_sem=route_send.at[1],
            recv_sem=route_recv.at[1],
            device_id=(gx, to_y, to_z),
            device_id_type=MESH,
        ).start()
        return carry

    lax.fori_loop(1, group, send_back, 0)
    interpolate(me)
    back = pltpu.make_async_copy(velocity.at[me], returned.at[me], own_sem.at[1])
    back.start()

    inner(half)
    for copy in second:
        copy.wait_recv()
    outer(half, final, 1)
    store = pltpu.make_async_copy(final, final_hbm, store_sem.at[0])
    store.start()

    back.wait()
    others = returned.at[pl.ds(0, group - 1)]
    pltpu.make_async_copy(others, others, route_recv.at[1]).wait()
    high, low = halves(returned[...].reshape(group * 8, 128))
    own_velocity[...] = dot(unpack[...], high) + dot(unpack[...], low)
    for b in range(blocks):
        lanes = slice(b * 128, (b + 1) * 128)
        moved[:, lanes] = (
            tracer[:, lanes] + ADVANCE * own_velocity[pl.ds(b, 3, stride=blocks), :]
        )
    store_moved = pltpu.make_async_copy(moved, moved_hbm, store_sem.at[1])
    store_moved.start()

    for copy in first + second:
        copy.wait_send()
    others = outgoing.at[pl.ds(0, group - 1)]
    pltpu.make_async_copy(others, others, route_send.at[0]).wait()
    others = velocity.at[pl.ds(0, group - 1)]
    pltpu.make_async_copy(others, others, route_send.at[1]).wait()
    store.wait()
    store_moved.wait()


def shards(sizes, fields, tracer_ref, host_element, block_owner):
    n_gx, n_gy, n_gz = sizes
    group = n_gy * n_gz
    blocks = block_owner.shape[0]
    planes, line, nodes = constants()
    any_space = pl.BlockSpec(memory_space=pl.ANY)
    return pl.pallas_call(
        functools.partial(body, (n_gx, n_gy, n_gz, blocks)),
        out_shape=(
            jax.ShapeDtypeStruct(fields.shape, F32),
            jax.ShapeDtypeStruct(tracer_ref.shape, F32),
        ),
        in_specs=[any_space] * 7,
        out_specs=(any_space, any_space),
        scratch_shapes=[
            pltpu.VMEM(fields.shape, F32),
            pltpu.VMEM(fields.shape, F32),
            pltpu.VMEM(fields.shape, F32),
            pltpu.VMEM(fields.shape, F32),
            pltpu.VMEM(tracer_ref.shape, F32),
            pltpu.VMEM((blocks, 128), jnp.int32),
            pltpu.VMEM((blocks, 1), jnp.int32),
            pltpu.VMEM(planes.shape, BF16),
            pltpu.VMEM(line.shape, BF16),
            pltpu.VMEM(nodes.shape, F32),
            pltpu.VMEM((2, 2, 5, 8, 128), F32),
            pltpu.VMEM((2, 8, 128), F32),
            pltpu.VMEM((2, 2, 5, 8, 128), F32),
            pltpu.VMEM((2, 2, 5, 8, 128), F32),
            pltpu.VMEM((2, 2, 8, 128), F32),
            pltpu.VMEM((4 * blocks, 128), F32),
            pltpu.VMEM((3 * blocks, 8 * group), BF16),
            pltpu.VMEM((group, 8, 128), F32),
            pltpu.VMEM((group, 8, 128), F32),
            pltpu.VMEM((group, 128, 256), BF16),
            pltpu.VMEM((group, 64, 256), F32),
            pltpu.VMEM((group, 8, 128), F32),
            pltpu.VMEM((group, 8, 128), F32),
            pltpu.VMEM((3 * blocks, 128), F32),
            pltpu.VMEM(tracer_ref.shape, F32),
            pltpu.SemaphoreType.DMA((7,)),
            pltpu.SemaphoreType.DMA((2, 6)),
            pltpu.SemaphoreType.DMA((2, 6)),
            pltpu.SemaphoreType.DMA((2,)),
            pltpu.SemaphoreType.DMA((2,)),
            pltpu.SemaphoreType.DMA((2,)),
            pltpu.SemaphoreType.DMA((2,)),
        ],
        compiler_params=pltpu.CompilerParams(
            collective_id=0, has_side_effects=True, vmem_limit_bytes=40 * 1024 * 1024
        ),
    )(
        fields,
        tracer_ref,
        host_element.reshape(blocks, 128),
        block_owner,
        jnp.asarray(planes),
        jnp.asarray(line),
        jnp.asarray(nodes),
    )


def solution(mesh):
    sizes = tuple(mesh.shape[axis] for axis in ("gx", "gy", "gz"))
    return jax.shard_map(
        functools.partial(shards, sizes),
        mesh=mesh,
        in_specs=(
            P(None, "gx", "gy", "gz"),
            P(None, ("gx", "gy", "gz")),
            P(("gx", "gy", "gz")),
            P(("gx", "gy", "gz"), None),
        ),
        out_specs=(P(None, "gx", "gy", "gz"), P(None, ("gx", "gy", "gz"))),
        check_vma=False,
    )
```

time: 97.7 us -> 33.4 us (0.34)
  the two profiles are of different devices: /device:TPU:129 before, /device:TPU:1 now
where the time goes in v1:
time: 33.4 us; the launch traced here: 33.1 us
  Pallas kernels  26.1 us (78%)
  local copies, waits for them, and re-layouts  6.28 us (19%)
  between operations  0.66 us (2%)
    pallas_call x1, Pallas kernels, shards(): pl.pallas_call(functools.partial(body, (n_gx, n_gy, n_gz, blocks)), out_s...  26.1 us
    unnamed x17, local copies, waits for them, and re-layouts  6.28 us

profile of v1, /device:TPU:1, one launch (start us, length us, event | category | flops | bytes accessed | tf_op | source)
XLA Modules:
  0.0 33.1 jit_solution(5427130996258756116)
XLA Ops:
  0.6 0.0 copy-start.6
  0.6 0.0 copy-start.5
  0.6 0.6 %copy-done.6 = s32[32,1]{0,1:T(1,128)S(1)} copy-done((s32[32,1]{0,1:T(1,128)S(1)}, s32[32,1]{0,1:T(1,128)}, u32[]{:S(2)}) %copy-start.6) | copy-done | bytes 152
  1.3 0.1 copy.9.owner_hbm
  1.4 0.0 copy-done.5
  1.4 0.0 copy-start
  1.4 0.9 %copy-done = f32[5,8,8,128]{3,2,1,0:T(8,128)S(1)} copy-done((f32[5,8,8,128]{3,2,1,0:T(8,128)S(1)}, f32[5,8,8,128]{3,2,1,0:T(8,128)}, u32[]{:S(2)}) %copy-start) | copy-done | bytes 163864
  2.3 0.0 copy-start.1
  2.3 0.9 %copy-done.1 = bf16[256,256]{1,0:T(8,128)(2,1)S(1)} copy-done((bf16[256,256]{1,0:T(8,128)(2,1)S(1)}, bf16[256,256]{1,0:T(8,128)(2,1)}, u32[]{:S(2)}) %copy-start.1) | copy-done | bytes 131096
  3.2 0.0 copy-start.2
  3.2 0.8 %copy-done.2 = f32[3,4096]{1,0:T(4,128)S(1)} copy-done((f32[3,4096]{1,0:T(4,128)S(1)}, f32[3,4096]{1,0:T(4,128)}, u32[]{:S(2)}) %copy-start.2) | copy-done | bytes 49176
  4.0 0.0 copy-start.3
  4.0 0.8 %copy-done.3 = bf16[128,192]{1,0:T(8,128)(2,1)S(1)} copy-done((bf16[128,192]{1,0:T(8,128)(2,1)S(1)}, bf16[128,192]{1,0:T(8,128)(2,1)}, u32[]{:S(2)}) %copy-start.3) | copy-done | bytes 49176
  4.9 0.0 copy-start.4
  4.9 0.8 %copy-done.4 = f32[8,8,128]{2,1,0:T(8,128)S(1)} copy-done((f32[8,8,128]{2,1,0:T(8,128)S(1)}, f32[8,8,128]{2,1,0:T(8,128)}, u32[]{:S(2)}) %copy-start.4) | copy-done | bytes 32792
  5.6 26.1 %shard_map.86 = (f32[5,8,8,128]{3,2,1,0:T(8,128)S(1)}, f32[3,4096]{1,0:T(4,128)S(1)}) custom-call(f32[5,8,8,128]{3,2,1,0:T(8,128)S(1)} %copy-done, f32[3,4096]{1,0:T(4,128)S(1)} %copy-done.2, s32[32,128]{1,0:T(8,128)S(1)} %bitcast.1, s32[32,1]{1,0:T(8,128)S(1)} %copy.9.owner_hbm, bf16[128,192]{1,0:T(8,128)(2,1)S(1)} %copy-done.3, ...), custom_call_target="tpu_custom_call" | custom-call | tf_op jit(solution)/shard_map/pallas_call | solution.py:429
  31.8 0.7 %copy.12 = f32[5,8,8,128]{3,2,1,0:T(8,128)} copy(f32[5,8,8,128]{3,2,1,0:T(8,128)S(1)} %get-tuple-element.4) | data formatting | bytes 327680
  32.4 0.6 %copy.13 = f32[3,4096]{1,0:T(4,128)} copy(f32[3,4096]{1,0:T(4,128)S(1)} %get-tuple-element.5) | data formatting | bytes 98304
Async XLA Ops:
  0.6 0.7 %copy-start.6 = (s32[32,1]{0,1:T(1,128)S(1)}, s32[32,1]{0,1:T(1,128)}, u32[]{:S(2)}) copy-start(s32[32,1]{0,1:T(1,128)} %param.10) | copy-start | bytes 388
  0.6 0.7 %copy-start.5 = (s32[4096]{0:T(1024)S(1)}, s32[4096]{0:T(1024)}, u32[]{:S(2)}) copy-start(s32[4096]{0:T(1024)} %param.9) | copy-start | bytes 49156
  1.4 0.9 %copy-start = (f32[5,8,8,128]{3,2,1,0:T(8,128)S(1)}, f32[5,8,8,128]{3,2,1,0:T(8,128)}, u32[]{:S(2)}) copy-start(f32[5,8,8,128]{3,2,1,0:T(8,128)} %fields_hbm.1) | copy-start | bytes 491524
  2.3 0.9 %copy-start.1 = (bf16[256,256]{1,0:T(8,128)(2,1)S(1)}, bf16[256,256]{1,0:T(8,128)(2,1)}, u32[]{:S(2)}) copy-start(bf16[256,256]{1,0:T(8,128)(2,1)} %constant.7.clone.line_hbm) | copy-start | bytes 393220
  3.2 0.8 %copy-start.2 = (f32[3,4096]{1,0:T(4,128)S(1)}, f32[3,4096]{1,0:T(4,128)}, u32[]{:S(2)}) copy-start(f32[3,4096]{1,0:T(4,128)} %tracer_hbm.1) | copy-start | bytes 147460
  4.0 0.8 %copy-start.3 = (bf16[128,192]{1,0:T(8,128)(2,1)S(1)}, bf16[128,192]{1,0:T(8,128)(2,1)}, u32[]{:S(2)}) copy-start(bf16[128,192]{1,0:T(8,128)(2,1)} %constant.6.clone.planes_hbm) | copy-start | bytes 147460
  4.9 0.8 %copy-start.4 = (f32[8,8,128]{2,1,0:T(8,128)S(1)}, f32[8,8,128]{2,1,0:T(8,128)}, u32[]{:S(2)}) copy-start(f32[8,8,128]{2,1,0:T(8,128)} %constant.8.clone.nodes_hbm) | copy-start | bytes 98308

commit v2 on v1

--- a/solution.py
+++ b/solution.py
@@ -52,33 +52,18 @@
     return matrix
 
 
-def split(matrix):
-    high = np.asarray(matrix, np.float32).astype(BF16)
-    low = (np.asarray(matrix, np.float64) - high.astype(np.float64)).astype(np.float32).astype(BF16)
-    return high, low
-
-
 def constants():
     element = -derivative_matrix()
     element[0, 0] -= LIFT
     element[7, 7] += LIFT
     element = element * TIME_STEP
     eye = np.eye(8)
-    both = np.concatenate([np.kron(element, eye), np.kron(eye, element)], 0)
-    high, low = split(both)
-    planes = np.concatenate([high, high, low], 1)
+    planes = np.concatenate([np.kron(element, eye), np.kron(eye, element)], 0)
     line = np.kron(np.eye(16), element)
     for e in range(1, 16):
         line[8 * e, 8 * e - 1] = LIFT * TIME_STEP
         line[8 * e - 1, 8 * e] = -LIFT * TIME_STEP
-    high, low = split(line.T)
-    line = np.concatenate(
-        [
-            np.concatenate([high, low], 1),
-            np.concatenate([high, np.zeros_like(low)], 1),
-        ],
-        0,
-    )
+    line = line.T
     points = gll_nodes()
     rows = np.zeros((8, 8))
     for n in range(8):
@@ -86,7 +71,24 @@
         rows[:7, n] = others
         rows[7, n] = 1.0 / np.prod([points[n] - other for other in others])
     nodes = np.broadcast_to(rows[:, :, None], (8, 8, 128)).astype(np.float32)
-    return planes, line, nodes
+    return planes.astype(np.float32), line.astype(np.float32), nodes
+
+
+def slab_offsets(rows, chips):
+    def distance(offset):
+        dy, dc, _ = offset
+        return min(dy, rows - dy) + min(dc, chips - dc)
+
+    offsets = sorted(
+        [(dy, dc, cx) for dy in range(rows) for dc in range(chips) for cx in range(2)],
+        key=lambda offset: (distance(offset),) + offset,
+    )
+    opposite = [offsets.index(((rows - dy) % rows, (chips - dc) % chips, cx)) for dy, dc, cx in offsets]
+    rings = [
+        [k for k, offset in enumerate(offsets) if distance(offset) == d]
+        for d in range(distance(offsets[-1]) + 1)
+    ]
+    return offsets, opposite, rings
 
 
 def halves(value):
@@ -108,18 +110,19 @@
     planes_hbm,
     line_hbm,
     nodes_hbm,
-    final_hbm,
-    moved_hbm,
+    final,
+    moved,
     state,
     half,
     part,
-    final,
     tracer,
     host,
     owner,
+    planes_f32,
+    line_f32,
+    nodes,
     planes,
     line,
-    nodes,
     y_out,
     z_out,
     x_in,
@@ -134,19 +137,17 @@
     velocity,
     returned,
     own_velocity,
-    moved,
     load_sem,
     halo_send,
     halo_recv,
     route_send,
     route_recv,
-    own_sem,
-    store_sem,
 ):
     n_gx, n_gy, n_gz, blocks = sizes
     group = n_gy * n_gz
     gx, gy, gz = lax.axis_index("gx"), lax.axis_index("gy"), lax.axis_index("gz")
     me = gy * n_gz + gz
+    offsets, opposite, rings = slab_offsets(n_gy, n_gz // 2)
 
     loads = [
         pltpu.make_async_copy(source, target, load_sem.at[i])
@@ -156,8 +157,8 @@
                 (owner_hbm, owner),
                 (tracer_hbm, tracer),
                 (host_hbm, host),
-                (planes_hbm, planes),
-                (line_hbm, line),
+                (planes_hbm, planes_f32),
+                (line_hbm, line_f32),
                 (nodes_hbm, nodes),
             ]
         )
@@ -165,24 +166,24 @@
     for load in loads:
         load.start()
 
+    chip, core = lax.div(gz, 2), lax.rem(gz, 2)
+    rows_to = [gy] + [lax.rem(gy + dy, n_gy) for dy in range(1, n_gy)]
+    chips_to = [chip] + [lax.rem(chip + dc, n_gz // 2) for dc in range(1, n_gz // 2)]
+    cores_to = [core, 1 - core]
+
     def peer(k):
-        to_y = lax.rem(gy + k // n_gz, n_gy)
-        to_z = lax.rem(gz + lax.rem(k, n_gz), n_gz)
-        return to_y, to_z
-
-    barrier = pltpu.get_barrier_semaphore()
-
-    def greet(k, carry):
-        to_y, to_z = peer(k)
-        pl.semaphore_signal(barrier, inc=1, device_id=(gx, to_y, to_z), device_id_type=MESH)
-        return carry
+        dy, dc, cx = offsets[k]
+        return rows_to[dy], chips_to[dc] * 2 + cores_to[cx]
 
     x_low, x_high = lax.rem(gx + n_gx - 1, n_gx), lax.rem(gx + 1, n_gx)
     y_low, y_high = lax.rem(gy + n_gy - 1, n_gy), lax.rem(gy + 1, n_gy)
     z_low, z_high = lax.rem(gz + n_gz - 1, n_gz), lax.rem(gz + 1, n_gz)
+
+    barrier = pltpu.get_barrier_semaphore()
+    for k in range(group - 1, 0, -1):
+        pl.semaphore_signal(barrier, inc=1, device_id=(gx,) + peer(k), device_id_type=MESH)
     for x in (x_low, x_high):
         pl.semaphore_signal(barrier, inc=1, device_id=(x, gy, gz), device_id_type=MESH)
-    lax.fori_loop(1, group, greet, 0)
 
     lane = lax.broadcasted_iota(jnp.int32, (8, 128), 1)
     sub = lax.broadcasted_iota(jnp.int32, (8, 128), 0)
@@ -263,7 +264,12 @@
 
     for load in loads[1:4]:
         load.wait()
-    owner_column = jnp.broadcast_to(owner[...].astype(F32), (blocks, 128))
+    square = jnp.broadcast_to(owner[...].astype(F32), (blocks, blocks))
+    diagonal = lax.broadcasted_iota(jnp.int32, (blocks, blocks), 0) == lax.broadcasted_iota(
+        jnp.int32, (blocks, blocks), 1
+    )
+    owner_column = jnp.sum(jnp.where(diagonal, square, 0.0), axis=1, keepdims=True)
+    owner_column = jnp.broadcast_to(owner_column, (blocks, 128))
     row = lax.broadcasted_iota(jnp.int32, (blocks, 128), 0)
     column = lax.broadcasted_iota(jnp.int32, (blocks, 128), 1)
     block_lane = lax.rem(column, blocks)
@@ -296,33 +302,46 @@
     )
     outgoing[...] = packed.reshape(group, 8, 128)
 
+    loads[4].wait()
+    loads[5].wait()
+    high, low = halves(planes_f32[...])
+    planes[...] = jnp.concatenate([high, high, low], 1)
+    high, low = halves(line_f32[...])
+    line[:128, :128] = high
+    line[128:, :128] = high
+    line[:128, 128:] = low
+    line[128:, 128:] = jnp.zeros_like(low)
+
     loads[0].wait()
     fill_halos(state, 0)
 
     pl.semaphore_wait(barrier, group + 1)
 
+    def send_block(k):
+        to_y, to_z = peer(k)
+        pltpu.make_async_remote_copy(
+            src_ref=outgoing.at[to_y * n_gz + to_z],
+            dst_ref=received.at[opposite[k]],
+            send_sem=route_send.at[0],
+            recv_sem=route_recv.at[0, ring_of(k)],
+            device_id=(gx, to_y, to_z),
+            device_id_type=MESH,
+        ).start()
+
+    def ring_of(k):
+        return [i for i, ring in enumerate(rings) if k in ring][0]
+
+    far = [k for ring in rings[3:][::-1] for k in ring]
+    near = [k for ring in rings[:3][::-1] for k in ring if k > 0]
+    for k in far:
+        send_block(k)
     first = halo_copies(state, 0)
     for copy in first:
         copy.start()
-
-    def send_block(k, carry):
-        to_y, to_z = peer(k)
-        pltpu.make_async_remote_copy(
-            src_ref=outgoing.at[to_y * n_gz + to_z],
-            dst_ref=received.at[me],
-            send_sem=route_send.at[0],
-            recv_sem=route_recv.at[0],
-            device_id=(gx, to_y, to_z),
-            device_id_type=MESH,
-        ).start()
-        return carry
-
-    lax.fori_loop(1, group, send_block, 0)
-    mine = pltpu.make_async_copy(outgoing.at[me], received.at[me], own_sem.at[0])
-    mine.start()
-
-    loads[4].wait()
-    loads[5].wait()
+    for k in near:
+        send_block(k)
+    received[0] = outgoing[me]
+
     inner(state)
     for copy in first:
         copy.wait_recv()
@@ -333,9 +352,8 @@
         copy.start()
 
     loads[6].wait()
-    mine.wait()
-    others = received.at[pl.ds(0, group - 1)]
-    pltpu.make_async_copy(others, others, route_recv.at[0]).wait()
+    table = half[0:3].reshape(192, 128).astype(BF16)
+    lower_half = jnp.where(lax.broadcasted_iota(jnp.int32, (16, 128), 0) >= 8, 1.0, 0.0)
 
     def lagrange(coordinate):
         value = nodes[7]
@@ -343,22 +361,19 @@
             value = value * (coordinate - nodes[k])
         return value
 
-    def weigh(s, carry):
+    def weigh(s):
         for a in range(2):
             lanes = slice(a * 128, (a + 1) * 128)
             coordinate = [received[s, 4 * a + c : 4 * a + c + 1, :] for c in range(4)]
             along = [lagrange(coordinate[c]) for c in range(3)]
-            for e in range(16):
-                z_weights[s, e * 8 : (e + 1) * 8, lanes] = jnp.where(
-                    coordinate[3] == float(e), along[2], 0.0
-                ).astype(BF16)
+            pair = jnp.concatenate([along[2], along[2]], 0).astype(BF16)
+            even = (coordinate[3] - lower_half).astype(BF16)
+            for e in range(8):
+                z_weights[s, e * 16 : (e + 1) * 16, lanes] = jnp.where(
+                    even == jnp.asarray(2 * e, BF16), pair, jnp.zeros_like(pair)
+                )
             for i in range(8):
                 xy_weights[s, i * 8 : (i + 1) * 8, lanes] = along[0][i : i + 1, :] * along[1]
-        return carry
-
-    lax.fori_loop(0, group, weigh, 0)
-
-    table = half[0:3].reshape(192, 128).astype(BF16)
 
     def interpolate(s):
         values = dot(table, z_weights[s])
@@ -371,35 +386,48 @@
             ]
             velocity[s, 4 * a : 4 * a + 4, :] = jnp.concatenate(rows + [jnp.zeros_like(rows[0])], 0)
 
-    def send_back(k, carry):
-        to_y, to_z = peer(k)
-        s = to_y * n_gz + to_z
-        interpolate(s)
-        pltpu.make_async_remote_copy(
-            src_ref=velocity.at[s],
-            dst_ref=returned.at[me],
-            send_sem=route_send.at[1],
-            recv_sem=route_recv.at[1],
-            device_id=(gx, to_y, to_z),
-            device_id_type=MESH,
-        ).start()
-        return carry
-
-    lax.fori_loop(1, group, send_back, 0)
-    interpolate(me)
-    back = pltpu.make_async_copy(velocity.at[me], returned.at[me], own_sem.at[1])
-    back.start()
+    def ring_bytes(ring, buffer):
+        return buffer.at[pl.ds(0, len([k for k in ring if k > 0]))]
+
+    def weigh_ring(i):
+        ring = rings[i]
+        span = ring_bytes(ring, received)
+        pltpu.make_async_copy(span, span, route_recv.at[0, i]).wait()
+
+        def step(s, carry):
+            weigh(s)
+            return carry
+
+        lax.fori_loop(ring[0], ring[-1] + 1, step, 0)
+
+    def answer_ring(i):
+        for k in rings[i]:
+            interpolate(k)
+        for k in rings[i]:
+            if k == 0:
+                returned[me] = velocity[0]
+                continue
+            pltpu.make_async_remote_copy(
+                src_ref=velocity.at[k],
+                dst_ref=returned.at[me],
+                send_sem=route_send.at[1],
+                recv_sem=route_recv.at[1, 0],
+                device_id=(gx,) + peer(k),
+                device_id_type=MESH,
+            ).start()
+
+    for i in range(len(rings)):
+        weigh_ring(i)
+    for i in range(len(rings)-1,-1,-1):
+        answer_ring(i)
 
     inner(half)
     for copy in second:
         copy.wait_recv()
     outer(half, final, 1)
-    store = pltpu.make_async_copy(final, final_hbm, store_sem.at[0])
-    store.start()
-
-    back.wait()
+
     others = returned.at[pl.ds(0, group - 1)]
-    pltpu.make_async_copy(others, others, route_recv.at[1]).wait()
+    pltpu.make_async_copy(others, others, route_recv.at[1, 0]).wait()
     high, low = halves(returned[...].reshape(group * 8, 128))
     own_velocity[...] = dot(unpack[...], high) + dot(unpack[...], low)
     for b in range(blocks):
@@ -407,8 +435,6 @@
         moved[:, lanes] = (
             tracer[:, lanes] + ADVANCE * own_velocity[pl.ds(b, 3, stride=blocks), :]
         )
-    store_moved = pltpu.make_async_copy(moved, moved_hbm, store_sem.at[1])
-    store_moved.start()
 
     for copy in first + second:
         copy.wait_send()
@@ -416,8 +442,6 @@
     pltpu.make_async_copy(others, others, route_send.at[0]).wait()
     others = velocity.at[pl.ds(0, group - 1)]
     pltpu.make_async_copy(others, others, route_send.at[1]).wait()
-    store.wait()
-    store_moved.wait()
 
 
 def shards(sizes, fields, tracer_ref, host_element, block_owner):
@@ -425,26 +449,37 @@
     group = n_gy * n_gz
     blocks = block_owner.shape[0]
     planes, line, nodes = constants()
-    any_space = pl.BlockSpec(memory_space=pl.ANY)
+    arrays = (
+        fields,
+        tracer_ref,
+        host_element.reshape(blocks, 128),
+        block_owner.reshape(1, blocks),
+        jnp.asarray(planes),
+        jnp.asarray(line),
+        jnp.asarray(nodes),
+    )
+    in_hbm = pl.BlockSpec(memory_space=pltpu.HBM)
+    in_vmem = pl.BlockSpec(memory_space=pltpu.VMEM)
     return pl.pallas_call(
         functools.partial(body, (n_gx, n_gy, n_gz, blocks)),
         out_shape=(
             jax.ShapeDtypeStruct(fields.shape, F32),
             jax.ShapeDtypeStruct(tracer_ref.shape, F32),
         ),
-        in_specs=[any_space] * 7,
-        out_specs=(any_space, any_space),
+        in_specs=[in_hbm] * len(arrays),
+        out_specs=(in_vmem, in_vmem),
         scratch_shapes=[
-            pltpu.VMEM(fields.shape, F32),
             pltpu.VMEM(fields.shape, F32),
             pltpu.VMEM(fields.shape, F32),
             pltpu.VMEM(fields.shape, F32),
             pltpu.VMEM(tracer_ref.shape, F32),
             pltpu.VMEM((blocks, 128), jnp.int32),
-            pltpu.VMEM((blocks, 1), jnp.int32),
-            pltpu.VMEM(planes.shape, BF16),
-            pltpu.VMEM(line.shape, BF16),
+            pltpu.VMEM((1, blocks), jnp.int32),
+            pltpu.VMEM(planes.shape, F32),
+            pltpu.VMEM(line.shape, F32),
             pltpu.VMEM(nodes.shape, F32),
+            pltpu.VMEM((128, 192), BF16),
+            pltpu.VMEM((256, 256), BF16),
             pltpu.VMEM((2, 2, 5, 8, 128), F32),
             pltpu.VMEM((2, 8, 128), F32),
             pltpu.VMEM((2, 2, 5, 8, 128), F32),
@@ -459,27 +494,16 @@
             pltpu.VMEM((group, 8, 128), F32),
             pltpu.VMEM((group, 8, 128), F32),
             pltpu.VMEM((3 * blocks, 128), F32),
-            pltpu.VMEM(tracer_ref.shape, F32),
-            pltpu.SemaphoreType.DMA((7,)),
+            pltpu.SemaphoreType.DMA((len(arrays),)),
             pltpu.SemaphoreType.DMA((2, 6)),
             pltpu.SemaphoreType.DMA((2, 6)),
             pltpu.SemaphoreType.DMA((2,)),
-            pltpu.SemaphoreType.DMA((2,)),
-            pltpu.SemaphoreType.DMA((2,)),
-            pltpu.SemaphoreType.DMA((2,)),
+            pltpu.SemaphoreType.DMA((2, 8)),
         ],
         compiler_params=pltpu.CompilerParams(
             collective_id=0, has_side_effects=True, vmem_limit_bytes=40 * 1024 * 1024
         ),
-    )(
-        fields,
-        tracer_ref,
-        host_element.reshape(blocks, 128),
-        block_owner,
-        jnp.asarray(planes),
-        jnp.asarray(line),
-        jnp.asarray(nodes),
-    )
+    )(*[pltpu.with_memory_space_constraint(array, pltpu.HBM) for array in arrays])
 
 
 def solution(mesh):

time: 33.4 us -> 23 us (0.69)
  Pallas kernels: 26.1 us -> 21 us
  local copies, waits for them, and re-layouts: 6.28 us -> 1.3 us
    pallas_call x1, Pallas kernels: 26.1 us -> 21 us  [shards(): pl.pallas_call(functools.partial(body, (n_gx, n_gy, n_gz, blocks)), out_s...]
    unnamed x17 -> x2, local copies, waits for them, and re-layouts: 6.28 us -> 1.3 us
where the time goes in v2:
time: 23 us; the launch traced here: 22.9 us
  Pallas kernels  21 us (91%)
  local copies, waits for them, and re-layouts  1.3 us (6%)
  between operations  0.64 us (3%)
    pallas_call x1, Pallas kernels, shards(): pl.pallas_call(functools.partial(body, (n_gx, n_gy, n_gz, blocks)), out_s...  21 us
    unnamed x2, local copies, waits for them, and re-layouts  1.3 us

profile of v2, /device:TPU:1, one launch (start us, length us, event | category | flops | bytes accessed | tf_op | source)
XLA Modules:
  0.0 22.9 jit_solution(15085274844978552866)
XLA Ops:
  0.6 21.0 %shard_map.86 = (f32[5,8,8,128]{3,2,1,0:T(8,128)S(1)}, f32[3,4096]{1,0:T(4,128)S(1)}) custom-call(f32[5,8,8,128]{3,2,1,0:T(8,128)} %fields_hbm.1, f32[3,4096]{1,0:T(4,128)} %tracer_hbm.1, s32[32,128]{1,0:T(8,128)} %bitcast.2, s32[1,32]{1,0:T(1,128)} %bitcast.3, f32[128,64]{1,0:T(8,128)} %constant.6.clone.planes_hbm, f32[128,128]{1,0:T(8,128)} %constant.7.clone.line_hbm, ...), custom_call_target="tpu_custom_call" | custom-call | tf_op jit(solution)/shard_map/pallas_call | solution.py:463
  21.6 0.7 %copy.11 = f32[5,8,8,128]{3,2,1,0:T(8,128)} copy(f32[5,8,8,128]{3,2,1,0:T(8,128)S(1)} %get-tuple-element.4) | data formatting | bytes 327680
  22.3 0.6 %copy.12 = f32[3,4096]{1,0:T(4,128)} copy(f32[3,4096]{1,0:T(4,128)S(1)} %get-tuple-element.5) | data formatting | bytes 98304

commit v3 on v2

--- a/solution.py
+++ b/solution.py
@@ -175,15 +175,43 @@
         dy, dc, cx = offsets[k]
         return rows_to[dy], chips_to[dc] * 2 + cores_to[cx]
 
-    x_low, x_high = lax.rem(gx + n_gx - 1, n_gx), lax.rem(gx + 1, n_gx)
+    has_low, has_high = gx > 0, gx < n_gx - 1
+    x_low, x_high = jnp.maximum(gx - 1, 0), jnp.minimum(gx + 1, n_gx - 1)
     y_low, y_high = lax.rem(gy + n_gy - 1, n_gy), lax.rem(gy + 1, n_gy)
     z_low, z_high = lax.rem(gz + n_gz - 1, n_gz), lax.rem(gz + 1, n_gz)
 
     barrier = pltpu.get_barrier_semaphore()
     for k in range(group - 1, 0, -1):
         pl.semaphore_signal(barrier, inc=1, device_id=(gx,) + peer(k), device_id_type=MESH)
-    for x in (x_low, x_high):
-        pl.semaphore_signal(barrier, inc=1, device_id=(x, gy, gz), device_id_type=MESH)
+    for x, present in ((x_low, has_low), (x_high, has_high)):
+
+        @pl.when(present)
+        def _(x=x):
+            pl.semaphore_signal(barrier, inc=1, device_id=(x, gy, gz), device_id_type=MESH)
+
+    for side, present in ((0, has_low), (1, has_high)):
+
+        @pl.when(jnp.logical_not(present))
+        def _(side=side):
+            for step in range(2):
+                x_in[step, side] = jnp.zeros_like(x_in[step, side])
+
+    sends_when = [has_low, has_high, None, None, None, None]
+    comes_when = [has_high, has_low, None, None, None, None]
+
+    def each(copies, conditions, act):
+        for copy, condition in zip(copies, conditions):
+            if condition is None:
+                act(copy)
+            else:
+                pl.when(condition)(functools.partial(act, copy))
+
+    def start_halos(copies):
+        each(copies, sends_when, lambda copy: copy.start())
+
+    def await_halos(copies):
+        each(copies, comes_when, lambda copy: copy.wait_recv())
+
 
     lane = lax.broadcasted_iota(jnp.int32, (8, 128), 1)
     sub = lax.broadcasted_iota(jnp.int32, (8, 128), 0)
@@ -315,7 +343,7 @@
     loads[0].wait()
     fill_halos(state, 0)
 
-    pl.semaphore_wait(barrier, group + 1)
+    pl.semaphore_wait(barrier, group - 1 + has_low.astype(jnp.int32) + has_high.astype(jnp.int32))
 
     def send_block(k):
         to_y, to_z = peer(k)
@@ -336,20 +364,17 @@
     for k in far:
         send_block(k)
     first = halo_copies(state, 0)
-    for copy in first:
-        copy.start()
+    start_halos(first)
     for k in near:
         send_block(k)
     received[0] = outgoing[me]
 
     inner(state)
-    for copy in first:
-        copy.wait_recv()
+    await_halos(first)
     outer(state, half, 0)
     fill_halos(half, 1)
     second = halo_copies(half, 1)
-    for copy in second:
-        copy.start()
+    start_halos(second)
 
     loads[6].wait()
     table = half[0:3].reshape(192, 128).astype(BF16)
@@ -416,14 +441,17 @@
                 device_id_type=MESH,
             ).start()
 
-    for i in range(len(rings)):
+    last = len(rings) - 1
+    for i in [0, 1]:
         weigh_ring(i)
-    for i in range(len(rings)-1,-1,-1):
+    for i in range(last, 1, -1):
+        weigh_ring(i)
         answer_ring(i)
+    for i in [1, 0]:
+        answer_ring(i)
 
     inner(half)
-    for copy in second:
-        copy.wait_recv()
+    await_halos(second)
     outer(half, final, 1)
 
     others = returned.at[pl.ds(0, group - 1)]
@@ -436,8 +464,8 @@
             tracer[:, lanes] + ADVANCE * own_velocity[pl.ds(b, 3, stride=blocks), :]
         )
 
-    for copy in first + second:
-        copy.wait_send()
+    for copies in (first, second):
+        each(copies, sends_when, lambda copy: copy.wait_send())
     others = outgoing.at[pl.ds(0, group - 1)]
     pltpu.make_async_copy(others, others, route_send.at[0]).wait()
     others = velocity.at[pl.ds(0, group - 1)]

time: 23 us -> 20.2 us (0.88)
  Pallas kernels: 21 us -> 18.1 us
    pallas_call x1, Pallas kernels: 21 us -> 18.1 us  [shards(): pl.pallas_call(functools.partial(body, (n_gx, n_gy, n_gz, blocks)), out_s...]
where the time goes in v3:
time: 20.2 us; the launch traced here: 20.1 us
  Pallas kernels  18.1 us (90%)
  local copies, waits for them, and re-layouts  1.3 us (6%)
  between operations  0.64 us (3%)
    pallas_call x1, Pallas kernels, shards(): pl.pallas_call(functools.partial(body, (n_gx, n_gy, n_gz, blocks)), out_s...  18.1 us
    unnamed x2, local copies, waits for them, and re-layouts  1.3 us

profile of v3, /device:TPU:1, one launch (start us, length us, event | category | flops | bytes accessed | tf_op | source)
XLA Modules:
  0.0 20.1 jit_solution(7520607264385552433)
XLA Ops:
  0.6 18.1 %shard_map.86 = (f32[5,8,8,128]{3,2,1,0:T(8,128)S(1)}, f32[3,4096]{1,0:T(4,128)S(1)}) custom-call(f32[5,8,8,128]{3,2,1,0:T(8,128)} %fields_hbm.1, f32[3,4096]{1,0:T(4,128)} %tracer_hbm.1, s32[32,128]{1,0:T(8,128)} %bitcast.2, s32[1,32]{1,0:T(1,128)} %bitcast.3, f32[128,64]{1,0:T(8,128)} %constant.6.clone.planes_hbm, f32[128,128]{1,0:T(8,128)} %constant.7.clone.line_hbm, ...), custom_call_target="tpu_custom_call" | custom-call | tf_op jit(solution)/shard_map/pallas_call | solution.py:491
  18.8 0.7 %copy.11 = f32[5,8,8,128]{3,2,1,0:T(8,128)} copy(f32[5,8,8,128]{3,2,1,0:T(8,128)S(1)} %get-tuple-element.4) | data formatting | bytes 327680
  19.5 0.6 %copy.12 = f32[3,4096]{1,0:T(4,128)} copy(f32[3,4096]{1,0:T(4,128)S(1)} %get-tuple-element.5) | data formatting | bytes 98304

commit v4 on v3

--- a/solution.py
+++ b/solution.py
@@ -111,11 +111,12 @@
     line_hbm,
     nodes_hbm,
     final,
-    moved,
+    returned,
+    tracer,
+    slots,
     state,
     half,
     part,
-    tracer,
     host,
     owner,
     planes_f32,
@@ -129,14 +130,11 @@
     y_in,
     z_in,
     payload,
-    unpack,
     outgoing,
     received,
     z_weights,
     xy_weights,
     velocity,
-    returned,
-    own_velocity,
     load_sem,
     halo_send,
     halo_recv,
@@ -163,9 +161,6 @@
             ]
         )
     ]
-    for load in loads:
-        load.start()
-
     chip, core = lax.div(gz, 2), lax.rem(gz, 2)
     rows_to = [gy] + [lax.rem(gy + dy, n_gy) for dy in range(1, n_gy)]
     chips_to = [chip] + [lax.rem(chip + dc, n_gz // 2) for dc in range(1, n_gz // 2)]
@@ -188,6 +183,9 @@
         @pl.when(present)
         def _(x=x):
             pl.semaphore_signal(barrier, inc=1, device_id=(x, gy, gz), device_id_type=MESH)
+
+    for i in (2, 1, 3, 0, 4, 5, 6):
+        loads[i].start()
 
     for side, present in ((0, has_low), (1, has_high)):
 
@@ -311,11 +309,7 @@
     )
     slot_lane = owner_lane * 8.0 + earlier_lane * 4.0
     slot_column = owner_column[:, :1] * 8.0 + earlier_column * 4.0
-    for c in range(3):
-        wide = lax.broadcasted_iota(jnp.int32, (blocks, group * 8), 1).astype(F32)
-        unpack[c * blocks : (c + 1) * blocks, :] = jnp.where(
-            wide == slot_column + float(c), 1.0, 0.0
-        ).astype(BF16)
+    slots[...] = jnp.broadcast_to(slot_column, (blocks, 128))
     for b in range(blocks):
         payload[pl.ds(b, 3, stride=blocks), :] = tracer[:, b * 128 : (b + 1) * 128]
     payload[3 * blocks :, :] = host[...].astype(F32)
@@ -397,18 +391,22 @@
                 z_weights[s, e * 16 : (e + 1) * 16, lanes] = jnp.where(
                     even == jnp.asarray(2 * e, BF16), pair, jnp.zeros_like(pair)
                 )
-            for i in range(8):
-                xy_weights[s, i * 8 : (i + 1) * 8, lanes] = along[0][i : i + 1, :] * along[1]
+            xy_weights[s, 0:8, lanes] = along[0]
+            xy_weights[s, 8:16, lanes] = along[1]
 
     def interpolate(s):
         values = dot(table, z_weights[s])
         for a in range(2):
             lanes = slice(a * 128, (a + 1) * 128)
-            weights = xy_weights[s, :, lanes]
-            rows = [
-                jnp.sum(values[c * 64 : (c + 1) * 64, lanes] * weights, axis=0, keepdims=True)
-                for c in range(3)
-            ]
+            rows = []
+            for c in range(3):
+                total = xy_weights[s, 0:1, lanes] * values[c * 64 : c * 64 + 8, lanes]
+                for i in range(1, 8):
+                    at = c * 64 + i * 8
+                    total = total + xy_weights[s, i : i + 1, lanes] * values[at : at + 8, lanes]
+                rows.append(
+                    jnp.sum(total * xy_weights[s, 8:16, lanes], axis=0, keepdims=True)
+                )
             velocity[s, 4 * a : 4 * a + 4, :] = jnp.concatenate(rows + [jnp.zeros_like(rows[0])], 0)
 
     def ring_bytes(ring, buffer):
@@ -456,20 +454,33 @@
 
     others = returned.at[pl.ds(0, group - 1)]
     pltpu.make_async_copy(others, others, route_recv.at[1, 0]).wait()
-    high, low = halves(returned[...].reshape(group * 8, 128))
-    own_velocity[...] = dot(unpack[...], high) + dot(unpack[...], low)
-    for b in range(blocks):
-        lanes = slice(b * 128, (b + 1) * 128)
-        moved[:, lanes] = (
-            tracer[:, lanes] + ADVANCE * own_velocity[pl.ds(b, 3, stride=blocks), :]
-        )
-
     for copies in (first, second):
         each(copies, sends_when, lambda copy: copy.wait_send())
     others = outgoing.at[pl.ds(0, group - 1)]
     pltpu.make_async_copy(others, others, route_send.at[0]).wait()
     others = velocity.at[pl.ds(0, group - 1)]
     pltpu.make_async_copy(others, others, route_send.at[1]).wait()
+
+
+def finish(final, returned, tracer, slots, final_hbm, moved_hbm, own_velocity, moved, store_sem):
+    store = pltpu.make_async_copy(final, final_hbm, store_sem.at[0])
+    store.start()
+    blocks, group = slots.shape[0], returned.shape[0]
+    high, low = halves(returned[...].reshape(group * 8, 128))
+    wide = lax.broadcasted_iota(jnp.int32, (blocks, group * 8), 1).astype(F32)
+    unpack = jnp.concatenate(
+        [jnp.where(wide == slots[:, :1] + float(c), 1.0, 0.0).astype(BF16) for c in range(3)], 0
+    )
+    own_velocity[...] = dot(unpack, high) + dot(unpack, low)
+    for b in range(blocks):
+        lanes = slice(b * 128, (b + 1) * 128)
+        moved[:, lanes] = (
+            tracer[:, lanes] + ADVANCE * own_velocity[pl.ds(b, 3, stride=blocks), :]
+        )
+    store_moved = pltpu.make_async_copy(moved, moved_hbm, store_sem.at[1])
+    store_moved.start()
+    store.wait()
+    store_moved.wait()
 
 
 def shards(sizes, fields, tracer_ref, host_element, block_owner):
@@ -488,19 +499,20 @@
     )
     in_hbm = pl.BlockSpec(memory_space=pltpu.HBM)
     in_vmem = pl.BlockSpec(memory_space=pltpu.VMEM)
-    return pl.pallas_call(
+    results = pl.pallas_call(
         functools.partial(body, (n_gx, n_gy, n_gz, blocks)),
         out_shape=(
             jax.ShapeDtypeStruct(fields.shape, F32),
+            jax.ShapeDtypeStruct((group, 8, 128), F32),
             jax.ShapeDtypeStruct(tracer_ref.shape, F32),
+            jax.ShapeDtypeStruct((blocks, 128), F32),
         ),
         in_specs=[in_hbm] * len(arrays),
-        out_specs=(in_vmem, in_vmem),
+        out_specs=(in_vmem,) * 4,
         scratch_shapes=[
             pltpu.VMEM(fields.shape, F32),
             pltpu.VMEM(fields.shape, F32),
             pltpu.VMEM(fields.shape, F32),
-            pltpu.VMEM(tracer_ref.shape, F32),
             pltpu.VMEM((blocks, 128), jnp.int32),
             pltpu.VMEM((1, blocks), jnp.int32),
             pltpu.VMEM(planes.shape, F32),
@@ -514,14 +526,11 @@
             pltpu.VMEM((2, 2, 5, 8, 128), F32),
             pltpu.VMEM((2, 2, 8, 128), F32),
             pltpu.VMEM((4 * blocks, 128), F32),
-            pltpu.VMEM((3 * blocks, 8 * group), BF16),
             pltpu.VMEM((group, 8, 128), F32),
             pltpu.VMEM((group, 8, 128), F32),
             pltpu.VMEM((group, 128, 256), BF16),
-            pltpu.VMEM((group, 64, 256), F32),
+            pltpu.VMEM((group, 16, 256), F32),
             pltpu.VMEM((group, 8, 128), F32),
-            pltpu.VMEM((group, 8, 128), F32),
-            pltpu.VMEM((3 * blocks, 128), F32),
             pltpu.SemaphoreType.DMA((len(arrays),)),
             pltpu.SemaphoreType.DMA((2, 6)),
             pltpu.SemaphoreType.DMA((2, 6)),
@@ -532,6 +541,21 @@
             collective_id=0, has_side_effects=True, vmem_limit_bytes=40 * 1024 * 1024
         ),
     )(*[pltpu.with_memory_space_constraint(array, pltpu.HBM) for array in arrays])
+    return pl.pallas_call(
+        finish,
+        out_shape=(
+            jax.ShapeDtypeStruct(fields.shape, F32),
+            jax.ShapeDtypeStruct(tracer_ref.shape, F32),
+        ),
+        in_specs=[in_vmem] * 4,
+        out_specs=(in_hbm, in_hbm),
+        scratch_shapes=[
+            pltpu.VMEM((3 * blocks, 128), F32),
+            pltpu.VMEM(tracer_ref.shape, F32),
+            pltpu.SemaphoreType.DMA((2,)),
+        ],
+        compiler_params=pltpu.CompilerParams(vmem_limit_bytes=2 * 1024 * 1024),
+    )(*results)
 
 
 def solution(mesh):

time: 20.2 us -> 19.5 us (0.965)
  local copies, waits for them, and re-layouts: 1.3 us -> 0 us
  Pallas kernels: 18.1 us -> 18.8 us
    unnamed x2 -> x0, local copies, waits for them, and re-layouts: 1.3 us -> none
    pallas_call x0 -> x1, Pallas kernels: none -> 0.9 us  [shards(): pl.pallas_call(finish, out_shape=(jax.ShapeDtypeStruct(fields.shape, F32)...]
    pallas_call x1, Pallas kernels: 18.1 us -> 17.9 us  [shards(): pl.pallas_call(functools.partial(body, (n_gx, n_gy, n_gz, blocks)), out_s...]
where the time goes in v4:
time: 19.5 us; the launch traced here: 19.4 us
  Pallas kernels  18.8 us (96%)
  between operations  0.64 us (3%)
    pallas_call x1, Pallas kernels, shards(): pl.pallas_call(functools.partial(body, (n_gx, n_gy, n_gz, blocks)), out_s...  17.9 us
    pallas_call x1, Pallas kernels, shards(): pl.pallas_call(finish, out_shape=(jax.ShapeDtypeStruct(fields.shape, F32)...  0.9 us

profile of v4, /device:TPU:1, one launch (start us, length us, event | category | flops | bytes accessed | tf_op | source)
XLA Modules:
  0.0 19.4 jit_solution(3567932704646410360)
XLA Ops:
  0.6 17.9 %shard_map.86 = (f32[5,8,8,128]{3,2,1,0:T(8,128)S(1)}, f32[32,8,128]{2,1,0:T(8,128)S(1)}, f32[3,4096]{1,0:T(4,128)S(1)}, f32[32,128]{1,0:T(8,128)S(1)}) custom-call(f32[5,8,8,128]{3,2,1,0:T(8,128)} %fields_hbm.1, f32[3,4096]{1,0:T(4,128)} %tracer_hbm.1, s32[32,128]{1,0:T(8,128)} %bitcast.2, s32[1,32]{1,0:T(1,128)} %bitcast.3, ...), custom_call_target="tpu_custom_call" | custom-call | tf_op jit(solution)/shard_map/pallas_call | solution.py:502
  18.5 0.9 %shard_map.87 = (f32[5,8,8,128]{3,2,1,0:T(8,128)}, f32[3,4096]{1,0:T(4,128)}) custom-call(f32[5,8,8,128]{3,2,1,0:T(8,128)S(1)} %get-tuple-element.6.final, f32[32,8,128]{2,1,0:T(8,128)S(1)} %get-tuple-element.7.returned, f32[3,4096]{1,0:T(4,128)S(1)} %get-tuple-element.8.tracer, f32[32,128]{1,0:T(8,128)S(1)} %get-tuple-element.9.slots), custom_call_target="tpu_custom_call" | custom-call | tf_op jit(solution)/shard_map/pallas_call | solution.py:544

commit v5 on v4

--- a/solution.py
+++ b/solution.py
@@ -76,14 +76,14 @@
 
 def slab_offsets(rows, chips):
     def distance(offset):
-        dy, dc, _ = offset
+        dy, dc = offset
         return min(dy, rows - dy) + min(dc, chips - dc)
 
     offsets = sorted(
-        [(dy, dc, cx) for dy in range(rows) for dc in range(chips) for cx in range(2)],
+        [(dy, dc) for dy in range(rows) for dc in range(chips)],
         key=lambda offset: (distance(offset),) + offset,
     )
-    opposite = [offsets.index(((rows - dy) % rows, (chips - dc) % chips, cx)) for dy, dc, cx in offsets]
+    opposite = [offsets.index(((rows - dy) % rows, (chips - dc) % chips)) for dy, dc in offsets]
     rings = [
         [k for k, offset in enumerate(offsets) if distance(offset) == d]
         for d in range(distance(offsets[-1]) + 1)
@@ -135,16 +135,18 @@
     z_weights,
     xy_weights,
     velocity,
+    sibling,
+    tables,
     load_sem,
     halo_send,
     halo_recv,
     route_send,
     route_recv,
+    table_sem,
 ):
     n_gx, n_gy, n_gz, blocks = sizes
-    group = n_gy * n_gz
+    group, chips = n_gy * n_gz, n_gy * (n_gz // 2)
     gx, gy, gz = lax.axis_index("gx"), lax.axis_index("gy"), lax.axis_index("gz")
-    me = gy * n_gz + gz
     offsets, opposite, rings = slab_offsets(n_gy, n_gz // 2)
 
     loads = [
@@ -164,11 +166,11 @@
     chip, core = lax.div(gz, 2), lax.rem(gz, 2)
     rows_to = [gy] + [lax.rem(gy + dy, n_gy) for dy in range(1, n_gy)]
     chips_to = [chip] + [lax.rem(chip + dc, n_gz // 2) for dc in range(1, n_gz // 2)]
-    cores_to = [core, 1 - core]
+    me = gy * (n_gz // 2) + chip
 
     def peer(k):
-        dy, dc, cx = offsets[k]
-        return rows_to[dy], chips_to[dc] * 2 + cores_to[cx]
+        dy, dc = offsets[k]
+        return rows_to[dy], chips_to[dc] * 2 + core
 
     has_low, has_high = gx > 0, gx < n_gx - 1
     x_low, x_high = jnp.maximum(gx - 1, 0), jnp.minimum(gx + 1, n_gx - 1)
@@ -176,8 +178,10 @@
     z_low, z_high = lax.rem(gz + n_gz - 1, n_gz), lax.rem(gz + 1, n_gz)
 
     barrier = pltpu.get_barrier_semaphore()
-    for k in range(group - 1, 0, -1):
+    for k in range(chips - 1, 0, -1):
         pl.semaphore_signal(barrier, inc=1, device_id=(gx,) + peer(k), device_id_type=MESH)
+    for z in (z_low, z_high):
+        pl.semaphore_signal(barrier, inc=1, device_id=(gx, gy, z), device_id_type=MESH)
     for x, present in ((x_low, has_low), (x_high, has_high)):
 
         @pl.when(present)
@@ -322,7 +326,7 @@
     packed = dot(
         jnp.concatenate([place, place], 1), jnp.concatenate([high, low], 0)
     )
-    outgoing[...] = packed.reshape(group, 8, 128)
+    outgoing[...] = packed.reshape(chips, 2, 8, 128)
 
     loads[4].wait()
     loads[5].wait()
@@ -337,12 +341,12 @@
     loads[0].wait()
     fill_halos(state, 0)
 
-    pl.semaphore_wait(barrier, group - 1 + has_low.astype(jnp.int32) + has_high.astype(jnp.int32))
+    pl.semaphore_wait(barrier, chips + 1 + has_low.astype(jnp.int32) + has_high.astype(jnp.int32))
 
     def send_block(k):
         to_y, to_z = peer(k)
         pltpu.make_async_remote_copy(
-            src_ref=outgoing.at[to_y * n_gz + to_z],
+            src_ref=outgoing.at[to_y * (n_gz // 2) + lax.div(to_z, 2)],
             dst_ref=received.at[opposite[k]],
             send_sem=route_send.at[0],
             recv_sem=route_recv.at[0, ring_of(k)],
@@ -367,11 +371,20 @@
     await_halos(first)
     outer(state, half, 0)
     fill_halos(half, 1)
+    partner = pltpu.make_async_remote_copy(
+        src_ref=half.at[pl.ds(0, 3)],
+        dst_ref=sibling,
+        send_sem=table_sem.at[0],
+        recv_sem=table_sem.at[1],
+        device_id=(gx, gy, chip * 2 + 1 - core),
+        device_id_type=MESH,
+    )
+    partner.start()
     second = halo_copies(half, 1)
     start_halos(second)
 
     loads[6].wait()
-    table = half[0:3].reshape(192, 128).astype(BF16)
+    tables[core] = half[0:3].reshape(192, 128).astype(BF16)
     lower_half = jnp.where(lax.broadcasted_iota(jnp.int32, (16, 128), 0) >= 8, 1.0, 0.0)
 
     def lagrange(coordinate):
@@ -380,10 +393,13 @@
             value = value * (coordinate - nodes[k])
         return value
 
-    def weigh(s):
+    def weigh(k, owner):
+        s = 2 * k + owner
         for a in range(2):
             lanes = slice(a * 128, (a + 1) * 128)
-            coordinate = [received[s, 4 * a + c : 4 * a + c + 1, :] for c in range(4)]
+            coordinate = [
+                received[k, owner, 4 * a + c : 4 * a + c + 1, :] for c in range(4)
+            ]
             along = [lagrange(coordinate[c]) for c in range(3)]
             pair = jnp.concatenate([along[2], along[2]], 0).astype(BF16)
             even = (coordinate[3] - lower_half).astype(BF16)
@@ -394,8 +410,9 @@
             xy_weights[s, 0:8, lanes] = along[0]
             xy_weights[s, 8:16, lanes] = along[1]
 
-    def interpolate(s):
-        values = dot(table, z_weights[s])
+    def interpolate(k, owner):
+        s = 2 * k + owner
+        values = dot(tables[owner], z_weights[s])
         for a in range(2):
             lanes = slice(a * 128, (a + 1) * 128)
             rows = []
@@ -407,25 +424,25 @@
                 rows.append(
                     jnp.sum(total * xy_weights[s, 8:16, lanes], axis=0, keepdims=True)
                 )
-            velocity[s, 4 * a : 4 * a + 4, :] = jnp.concatenate(rows + [jnp.zeros_like(rows[0])], 0)
-
-    def ring_bytes(ring, buffer):
-        return buffer.at[pl.ds(0, len([k for k in ring if k > 0]))]
+            velocity[k, owner, 4 * a : 4 * a + 4, :] = jnp.concatenate(rows + [jnp.zeros_like(rows[0])], 0)
 
     def weigh_ring(i):
         ring = rings[i]
-        span = ring_bytes(ring, received)
-        pltpu.make_async_copy(span, span, route_recv.at[0, i]).wait()
-
-        def step(s, carry):
-            weigh(s)
+        if i > 0:
+            span = received.at[pl.ds(0, len(ring))]
+            pltpu.make_async_copy(span, span, route_recv.at[0, i]).wait()
+
+        def step(k, carry):
+            weigh(k, 0)
+            weigh(k, 1)
             return carry
 
         lax.fori_loop(ring[0], ring[-1] + 1, step, 0)
 
     def answer_ring(i):
         for k in rings[i]:
-            interpolate(k)
+            interpolate(k, 0)
+            interpolate(k, 1)
         for k in rings[i]:
             if k == 0:
                 returned[me] = velocity[0]
@@ -442,6 +459,8 @@
     last = len(rings) - 1
     for i in [0, 1]:
         weigh_ring(i)
+    partner.wait_recv()
+    tables[1 - core] = sibling[...].reshape(192, 128).astype(BF16)
     for i in range(last, 1, -1):
         weigh_ring(i)
         answer_ring(i)
@@ -452,20 +471,21 @@
     await_halos(second)
     outer(half, final, 1)
 
-    others = returned.at[pl.ds(0, group - 1)]
+    others = returned.at[pl.ds(0, chips - 1)]
     pltpu.make_async_copy(others, others, route_recv.at[1, 0]).wait()
+    partner.wait_send()
     for copies in (first, second):
         each(copies, sends_when, lambda copy: copy.wait_send())
-    others = outgoing.at[pl.ds(0, group - 1)]
+    others = outgoing.at[pl.ds(0, chips - 1)]
     pltpu.make_async_copy(others, others, route_send.at[0]).wait()
-    others = velocity.at[pl.ds(0, group - 1)]
+    others = velocity.at[pl.ds(0, chips - 1)]
     pltpu.make_async_copy(others, others, route_send.at[1]).wait()
 
 
 def finish(final, returned, tracer, slots, final_hbm, moved_hbm, own_velocity, moved, store_sem):
     store = pltpu.make_async_copy(final, final_hbm, store_sem.at[0])
     store.start()
-    blocks, group = slots.shape[0], returned.shape[0]
+    blocks, group = slots.shape[0], 2 * returned.shape[0]
     high, low = halves(returned[...].reshape(group * 8, 128))
     wide = lax.broadcasted_iota(jnp.int32, (blocks, group * 8), 1).astype(F32)
     unpack = jnp.concatenate(
@@ -485,7 +505,7 @@
 
 def shards(sizes, fields, tracer_ref, host_element, block_owner):
     n_gx, n_gy, n_gz = sizes
-    group = n_gy * n_gz
+    group, chips = n_gy * n_gz, n_gy * (n_gz // 2)
     blocks = block_owner.shape[0]
     planes, line, nodes = constants()
     arrays = (
@@ -503,7 +523,7 @@
         functools.partial(body, (n_gx, n_gy, n_gz, blocks)),
         out_shape=(
             jax.ShapeDtypeStruct(fields.shape, F32),
-            jax.ShapeDtypeStruct((group, 8, 128), F32),
+            jax.ShapeDtypeStruct((chips, 2, 8, 128), F32),
             jax.ShapeDtypeStruct(tracer_ref.shape, F32),
             jax.ShapeDtypeStruct((blocks, 128), F32),
         ),
@@ -526,16 +546,19 @@
             pltpu.VMEM((2, 2, 5, 8, 128), F32),
             pltpu.VMEM((2, 2, 8, 128), F32),
             pltpu.VMEM((4 * blocks, 128), F32),
-            pltpu.VMEM((group, 8, 128), F32),
-            pltpu.VMEM((group, 8, 128), F32),
+            pltpu.VMEM((chips, 2, 8, 128), F32),
+            pltpu.VMEM((chips, 2, 8, 128), F32),
             pltpu.VMEM((group, 128, 256), BF16),
             pltpu.VMEM((group, 16, 256), F32),
-            pltpu.VMEM((group, 8, 128), F32),
+            pltpu.VMEM((chips, 2, 8, 128), F32),
+            pltpu.VMEM((3, 8, 8, 128), F32),
+            pltpu.VMEM((2, 192, 128), BF16),
             pltpu.SemaphoreType.DMA((len(arrays),)),
             pltpu.SemaphoreType.DMA((2, 6)),
             pltpu.SemaphoreType.DMA((2, 6)),
             pltpu.SemaphoreType.DMA((2,)),
             pltpu.SemaphoreType.DMA((2, 8)),
+            pltpu.SemaphoreType.DMA((2,)),
         ],
         compiler_params=pltpu.CompilerParams(
             collective_id=0, has_side_effects=True, vmem_limit_bytes=40 * 1024 * 1024

time: 19.5 us -> 19 us (0.974)
  Pallas kernels: 18.8 us -> 18.3 us
    pallas_call x1, Pallas kernels: 17.9 us -> 17.4 us  [shards(): pl.pallas_call(functools.partial(body, (n_gx, n_gy, n_gz, blocks)), out_s...]
where the time goes in v5:
time: 19 us; the launch traced here: 18.9 us
  Pallas kernels  18.3 us (96%)
  between operations  0.64 us (3%)
    pallas_call x1, Pallas kernels, shards(): pl.pallas_call(functools.partial(body, (n_gx, n_gy, n_gz, blocks)), out_s...  17.4 us
    pallas_call x1, Pallas kernels, shards(): pl.pallas_call(finish, out_shape=(jax.ShapeDtypeStruct(fields.shape, F32)...  0.9 us

profile of v5, /device:TPU:1, one launch (start us, length us, event | category | flops | bytes accessed | tf_op | source)
XLA Modules:
  0.0 18.9 jit_solution(2293244524302464895)
XLA Ops:
  0.6 17.4 %shard_map.86 = (f32[5,8,8,128]{3,2,1,0:T(8,128)S(1)}, f32[16,2,8,128]{3,2,1,0:T(8,128)S(1)}, f32[3,4096]{1,0:T(4,128)S(1)}, f32[32,128]{1,0:T(8,128)S(1)}) custom-call(f32[5,8,8,128]{3,2,1,0:T(8,128)} %fields_hbm.1, f32[3,4096]{1,0:T(4,128)} %tracer_hbm.1, s32[32,128]{1,0:T(8,128)} %bitcast.2, s32[1,32]{1,0:T(1,128)} %bitcast.3, ...), custom_call_target="tpu_custom_call" | custom-call | tf_op jit(solution)/shard_map/pallas_call | solution.py:522
  18.0 0.9 %shard_map.87 = (f32[5,8,8,128]{3,2,1,0:T(8,128)}, f32[3,4096]{1,0:T(4,128)}) custom-call(f32[5,8,8,128]{3,2,1,0:T(8,128)S(1)} %get-tuple-element.6.final, f32[16,2,8,128]{3,2,1,0:T(8,128)S(1)} %get-tuple-element.7.returned, f32[3,4096]{1,0:T(4,128)S(1)} %get-tuple-element.8.tracer, f32[32,128]{1,0:T(8,128)S(1)} %get-tuple-element.9.slots), custom_call_target="tpu_custom_call" | custom-call | tf_op jit(solution)/shard_map/pallas_call | solution.py:567

commit v6 on v5

--- a/solution.py
+++ b/solution.py
@@ -64,14 +64,7 @@
         line[8 * e, 8 * e - 1] = LIFT * TIME_STEP
         line[8 * e - 1, 8 * e] = -LIFT * TIME_STEP
     line = line.T
-    points = gll_nodes()
-    rows = np.zeros((8, 8))
-    for n in range(8):
-        others = [points[m] for m in range(8) if m != n]
-        rows[:7, n] = others
-        rows[7, n] = 1.0 / np.prod([points[n] - other for other in others])
-    nodes = np.broadcast_to(rows[:, :, None], (8, 8, 128)).astype(np.float32)
-    return planes.astype(np.float32), line.astype(np.float32), nodes
+    return planes.astype(np.float32), line.astype(np.float32)
 
 
 def slab_offsets(rows, chips):
@@ -79,14 +72,16 @@
         dy, dc = offset
         return min(dy, rows - dy) + min(dc, chips - dc)
 
+    every = [(dy, dc) for dy in range(rows) for dc in range(chips)]
+    farthest = max(distance(offset) for offset in every)
     offsets = sorted(
-        [(dy, dc) for dy in range(rows) for dc in range(chips)],
-        key=lambda offset: (distance(offset),) + offset,
+        every,
+        key=lambda offset: (0.5 if distance(offset) == farthest else distance(offset),) + offset,
     )
     opposite = [offsets.index(((rows - dy) % rows, (chips - dc) % chips)) for dy, dc in offsets]
     rings = [
         [k for k, offset in enumerate(offsets) if distance(offset) == d]
-        for d in range(distance(offsets[-1]) + 1)
+        for d in range(farthest + 1)
     ]
     return offsets, opposite, rings
 
@@ -109,7 +104,6 @@
     owner_hbm,
     planes_hbm,
     line_hbm,
-    nodes_hbm,
     final,
     returned,
     tracer,
@@ -121,7 +115,6 @@
     owner,
     planes_f32,
     line_f32,
-    nodes,
     planes,
     line,
     y_out,
@@ -133,7 +126,7 @@
     outgoing,
     received,
     z_weights,
-    xy_weights,
+    factors,
     velocity,
     sibling,
     tables,
@@ -159,7 +152,6 @@
                 (host_hbm, host),
                 (planes_hbm, planes_f32),
                 (line_hbm, line_f32),
-                (nodes_hbm, nodes),
             ]
         )
     ]
@@ -188,7 +180,7 @@
         def _(x=x):
             pl.semaphore_signal(barrier, inc=1, device_id=(x, gy, gz), device_id_type=MESH)
 
-    for i in (2, 1, 3, 0, 4, 5, 6):
+    for i in (2, 1, 3, 0, 4, 5):
         loads[i].start()
 
     for side, present in ((0, has_low), (1, has_high)):
@@ -270,7 +262,7 @@
     y_next = jnp.where(sub == 7, jnp.where(gy == n_gy - 1, 0.0, -lift), 0.0)
     z_side = jnp.where(lane == 0, lift, 0.0) + jnp.where(lane == 127, -lift, 0.0)
 
-    def outer(source, target, step):
+    def outer(source, target, step, which=range(5)):
         merged = jnp.where(
             lane % 2 == 0,
             pltpu.roll(z_in[step, 1], 127, 1),
@@ -280,7 +272,7 @@
             wind = [source[d, x] for d in range(3)]
             y_wind = (wind[1] * y_prev, wind[1] * y_next)
             z_wind = wind[2] * z_side
-            for f in range(5):
+            for f in which:
                 at = f * 8 + x
                 total = part[f, x]
                 if x == 0:
@@ -294,7 +286,8 @@
 
     for load in loads[1:4]:
         load.wait()
-    square = jnp.broadcast_to(owner[...].astype(F32), (blocks, blocks))
+    place_of = jnp.bitwise_xor(owner[...], core).astype(F32)
+    square = jnp.broadcast_to(place_of, (blocks, blocks))
     diagonal = lax.broadcasted_iota(jnp.int32, (blocks, blocks), 0) == lax.broadcasted_iota(
         jnp.int32, (blocks, blocks), 1
     )
@@ -326,7 +319,7 @@
     packed = dot(
         jnp.concatenate([place, place], 1), jnp.concatenate([high, low], 0)
     )
-    outgoing[...] = packed.reshape(chips, 2, 8, 128)
+    outgoing[...] = packed
 
     loads[4].wait()
     loads[5].wait()
@@ -346,8 +339,10 @@
     def send_block(k):
         to_y, to_z = peer(k)
         pltpu.make_async_remote_copy(
-            src_ref=outgoing.at[to_y * (n_gz // 2) + lax.div(to_z, 2)],
-            dst_ref=received.at[opposite[k]],
+            src_ref=outgoing.at[
+                pl.ds(pl.multiple_of((to_y * (n_gz // 2) + lax.div(to_z, 2)) * 16, 16), 16)
+            ],
+            dst_ref=received.at[pl.ds(opposite[k] * 16, 16)],
             send_sem=route_send.at[0],
             recv_sem=route_recv.at[0, ring_of(k)],
             device_id=(gx, to_y, to_z),
@@ -359,18 +354,17 @@
 
     far = [k for ring in rings[3:][::-1] for k in ring]
     near = [k for ring in rings[:3][::-1] for k in ring if k > 0]
+    first = halo_copies(state, 0)
+    start_halos(first)
     for k in far:
         send_block(k)
-    first = halo_copies(state, 0)
-    start_halos(first)
     for k in near:
         send_block(k)
-    received[0] = outgoing[me]
+    received[0:16, :] = outgoing[pl.ds(pl.multiple_of(me * 16, 16), 16), :]
 
     inner(state)
     await_halos(first)
-    outer(state, half, 0)
-    fill_halos(half, 1)
+    outer(state, half, 0, range(3))
     partner = pltpu.make_async_remote_copy(
         src_ref=half.at[pl.ds(0, 3)],
         dst_ref=sibling,
@@ -380,70 +374,86 @@
         device_id_type=MESH,
     )
     partner.start()
+    outer(state, half, 0, range(3, 5))
+    fill_halos(half, 1)
     second = halo_copies(half, 1)
     start_halos(second)
 
-    loads[6].wait()
-    tables[core] = half[0:3].reshape(192, 128).astype(BF16)
+    tables[0] = half[0:3].reshape(192, 128).astype(BF16)
     lower_half = jnp.where(lax.broadcasted_iota(jnp.int32, (16, 128), 0) >= 8, 1.0, 0.0)
 
+    points = gll_nodes()
+    scales = [
+        float(1.0 / np.prod([points[n] - points[m] for m in range(8) if m != n])) for n in range(8)
+    ]
+
     def lagrange(coordinate):
-        value = nodes[7]
-        for k in range(7):
-            value = value * (coordinate - nodes[k])
-        return value
-
-    def weigh(k, owner):
-        s = 2 * k + owner
-        for a in range(2):
-            lanes = slice(a * 128, (a + 1) * 128)
-            coordinate = [
-                received[k, owner, 4 * a + c : 4 * a + c + 1, :] for c in range(4)
-            ]
-            along = [lagrange(coordinate[c]) for c in range(3)]
-            pair = jnp.concatenate([along[2], along[2]], 0).astype(BF16)
-            even = (coordinate[3] - lower_half).astype(BF16)
+        steps = [coordinate - float(points[m]) for m in range(8)]
+        before, after = [None, steps[0]], [None, steps[7]]
+        for m in range(1, 7):
+            before.append(before[-1] * steps[m])
+            after.append(after[-1] * steps[7 - m])
+        after = after[::-1]
+        values = [after[0]] + [before[n] * after[n] for n in range(1, 7)] + [before[7]]
+        return [value * scale for value, scale in zip(values, scales)]
+
+    def weigh(p):
+        for c in range(3):
+            for n, value in enumerate(lagrange(received[pl.ds(p * 32 + c, 8, stride=4), :])):
+                factors[pl.ds(pl.multiple_of(p * 192 + c * 64 + n * 8, 8), 8), :] = value
+        for at in range(8):
+            lanes = slice((at % 2) * 128, (at % 2 + 1) * 128)
+            along = factors[pl.ds(p * 192 + 128 + at, 8, stride=8), :]
+            pair = jnp.concatenate([along, along], 0).astype(BF16)
+            even = (received[pl.ds(p * 32 + at * 4 + 3, 1), :] - lower_half).astype(BF16)
             for e in range(8):
-                z_weights[s, e * 16 : (e + 1) * 16, lanes] = jnp.where(
+                z_weights[p * 4 + at // 2, e * 16 : (e + 1) * 16, lanes] = jnp.where(
                     even == jnp.asarray(2 * e, BF16), pair, jnp.zeros_like(pair)
                 )
-            xy_weights[s, 0:8, lanes] = along[0]
-            xy_weights[s, 8:16, lanes] = along[1]
 
     def interpolate(k, owner):
         s = 2 * k + owner
         values = dot(tables[owner], z_weights[s])
         for a in range(2):
             lanes = slice(a * 128, (a + 1) * 128)
+            base = (k // 2) * 192 + (k % 2) * 4 + owner * 2 + a
+            across = factors[pl.ds(base + 64, 8, stride=8), :]
             rows = []
             for c in range(3):
-                total = xy_weights[s, 0:1, lanes] * values[c * 64 : c * 64 + 8, lanes]
-                for i in range(1, 8):
+                total = None
+                for i in range(8):
                     at = c * 64 + i * 8
-                    total = total + xy_weights[s, i : i + 1, lanes] * values[at : at + 8, lanes]
-                rows.append(
-                    jnp.sum(total * xy_weights[s, 8:16, lanes], axis=0, keepdims=True)
-                )
+                    term = factors[base + i * 8 : base + i * 8 + 1, :] * values[at : at + 8, lanes]
+                    total = term if total is None else total + term
+                rows.append(jnp.sum(total * across, axis=0, keepdims=True))
             velocity[k, owner, 4 * a : 4 * a + 4, :] = jnp.concatenate(rows + [jnp.zeros_like(rows[0])], 0)
 
+    def await_ring(i):
+        span = received.at[pl.ds(0, 16 * len(rings[i]))]
+        pltpu.make_async_copy(span, span, route_recv.at[0, i]).wait()
+
+    def weigh_pairs(first_pair, end_pair):
+        def step(p, carry):
+            weigh(p)
+            return carry
+
+        lax.fori_loop(first_pair, end_pair, step, 0)
+
     def weigh_ring(i):
-        ring = rings[i]
-        if i > 0:
-            span = received.at[pl.ds(0, len(ring))]
-            pltpu.make_async_copy(span, span, route_recv.at[0, i]).wait()
-
-        def step(k, carry):
-            weigh(k, 0)
-            weigh(k, 1)
-            return carry
-
-        lax.fori_loop(ring[0], ring[-1] + 1, step, 0)
-
-    def answer_ring(i):
-        for k in rings[i]:
-            interpolate(k, 0)
-            interpolate(k, 1)
-        for k in rings[i]:
+        await_ring(i)
+        if i == len(rings) - 1:
+            weigh_pairs(0, 1)
+        else:
+            weigh_pairs(rings[i][0] // 2, (rings[i][-1] + 1) // 2)
+
+    def apply(table, *which):
+        for i in which:
+            for k in rings[i]:
+                interpolate(k, table)
+
+    def answer(*which):
+        ks = [k for i in which for k in rings[i]]
+        for k in ks:
             if k == 0:
                 returned[me] = velocity[0]
                 continue
@@ -457,15 +467,25 @@
             ).start()
 
     last = len(rings) - 1
-    for i in [0, 1]:
+    far_rings = tuple(range(last, max(last - 2, 1), -1))
+    middle = tuple(range(min(far_rings) - 1, 1, -1))
+    weigh_ring(1)
+    apply(0, 1)
+    for i in far_rings[::-1]:
         weigh_ring(i)
+    apply(0, *far_rings)
     partner.wait_recv()
-    tables[1 - core] = sibling[...].reshape(192, 128).astype(BF16)
-    for i in range(last, 1, -1):
+    tables[1] = sibling[...].reshape(192, 128).astype(BF16)
+    apply(1, *far_rings)
+    answer(*far_rings)
+    for i in middle:
         weigh_ring(i)
-        answer_ring(i)
-    for i in [1, 0]:
-        answer_ring(i)
+        apply(0, i)
+        apply(1, i)
+        answer(i)
+    apply(0, 0)
+    apply(1, 1, 0)
+    answer(1, 0)
 
     inner(half)
     await_halos(second)
@@ -476,7 +496,7 @@
     partner.wait_send()
     for copies in (first, second):
         each(copies, sends_when, lambda copy: copy.wait_send())
-    others = outgoing.at[pl.ds(0, chips - 1)]
+    others = outgoing.at[pl.ds(0, 16 * (chips - 1))]
     pltpu.make_async_copy(others, others, route_send.at[0]).wait()
     others = velocity.at[pl.ds(0, chips - 1)]
     pltpu.make_async_copy(others, others, route_send.at[1]).wait()
@@ -507,7 +527,7 @@
     n_gx, n_gy, n_gz = sizes
     group, chips = n_gy * n_gz, n_gy * (n_gz // 2)
     blocks = block_owner.shape[0]
-    planes, line, nodes = constants()
+    planes, line = constants()
     arrays = (
         fields,
         tracer_ref,
@@ -515,7 +535,6 @@
         block_owner.reshape(1, blocks),
         jnp.asarray(planes),
         jnp.asarray(line),
-        jnp.asarray(nodes),
     )
     in_hbm = pl.BlockSpec(memory_space=pltpu.HBM)
     in_vmem = pl.BlockSpec(memory_space=pltpu.VMEM)
@@ -537,7 +556,6 @@
             pltpu.VMEM((1, blocks), jnp.int32),
             pltpu.VMEM(planes.shape, F32),
             pltpu.VMEM(line.shape, F32),
-            pltpu.VMEM(nodes.shape, F32),
             pltpu.VMEM((128, 192), BF16),
             pltpu.VMEM((256, 256), BF16),
             pltpu.VMEM((2, 2, 5, 8, 128), F32),
@@ -546,10 +564,10 @@
             pltpu.VMEM((2, 2, 5, 8, 128), F32),
             pltpu.VMEM((2, 2, 8, 128), F32),
             pltpu.VMEM((4 * blocks, 128), F32),
-            pltpu.VMEM((chips, 2, 8, 128), F32),
-            pltpu.VMEM((chips, 2, 8, 128), F32),
+            pltpu.VMEM((group * 8, 128), F32),
+            pltpu.VMEM((group * 8, 128), F32),
             pltpu.VMEM((group, 128, 256), BF16),
-            pltpu.VMEM((group, 16, 256), F32),
+            pltpu.VMEM((chips // 2 * 192, 128), F32),
             pltpu.VMEM((chips, 2, 8, 128), F32),
             pltpu.VMEM((3, 8, 8, 128), F32),
             pltpu.VMEM((2, 192, 128), BF16),

time: 19 us -> 18.8 us (0.989)
  the two profiles are of different devices: /device:TPU:1 before, /device:TPU:64 now
where the time goes in v6:
time: 18.8 us; the launch traced here: 18.7 us
  Pallas kernels  18.1 us (96%)
  between operations  0.64 us (3%)
    pallas_call x1, Pallas kernels, shards(): pl.pallas_call(functools.partial(body, (n_gx, n_gy, n_gz, blocks)), out_s...  17.2 us
    pallas_call x1, Pallas kernels, shards(): pl.pallas_call(finish, out_shape=(jax.ShapeDtypeStruct(fields.shape, F32)...  0.9 us

profile of v6, /device:TPU:64, one launch (start us, length us, event | category | flops | bytes accessed | tf_op | source)
XLA Modules:
  0.0 18.7 jit_solution(12481497230133861831)
XLA Ops:
  0.6 17.2 %shard_map.77 = (f32[5,8,8,128]{3,2,1,0:T(8,128)S(1)}, f32[16,2,8,128]{3,2,1,0:T(8,128)S(1)}, f32[3,4096]{1,0:T(4,128)S(1)}, f32[32,128]{1,0:T(8,128)S(1)}) custom-call(f32[5,8,8,128]{3,2,1,0:T(8,128)} %fields_hbm.1, f32[3,4096]{1,0:T(4,128)} %tracer_hbm.1, s32[32,128]{1,0:T(8,128)} %bitcast.2, s32[1,32]{1,0:T(1,128)} %bitcast.3, ...), custom_call_target="tpu_custom_call" | custom-call | tf_op jit(solution)/shard_map/pallas_call | solution.py:541
  17.8 0.9 %shard_map.78 = (f32[5,8,8,128]{3,2,1,0:T(8,128)}, f32[3,4096]{1,0:T(4,128)}) custom-call(f32[5,8,8,128]{3,2,1,0:T(8,128)S(1)} %get-tuple-element.6.final, f32[16,2,8,128]{3,2,1,0:T(8,128)S(1)} %get-tuple-element.7.returned, f32[3,4096]{1,0:T(4,128)S(1)} %get-tuple-element.8.tracer, f32[32,128]{1,0:T(8,128)S(1)} %get-tuple-element.9.slots), custom_call_target="tpu_custom_call" | custom-call | tf_op jit(solution)/shard_map/pallas_call | solution.py:585

commit v7 on v6

--- a/solution.py
+++ b/solution.py
@@ -309,13 +309,13 @@
     slots[...] = jnp.broadcast_to(slot_column, (blocks, 128))
     for b in range(blocks):
         payload[pl.ds(b, 3, stride=blocks), :] = tracer[:, b * 128 : (b + 1) * 128]
-    payload[3 * blocks :, :] = host[...].astype(F32)
+    payload[3 * blocks : 4 * blocks, :] = host[...].astype(F32)
     width = 4 * blocks
     tall = lax.broadcasted_iota(jnp.int32, (group * 8, width), 0).astype(F32)
     part_lane = lax.broadcasted_iota(jnp.int32, (1, width), 1) // blocks
     target_row = slot_lane[:, :width] + part_lane.astype(F32)
     place = jnp.where(tall == target_row, 1.0, 0.0).astype(BF16)
-    high, low = halves(payload[...])
+    high, low = halves(payload[0 : 4 * blocks, :])
     packed = dot(
         jnp.concatenate([place, place], 1), jnp.concatenate([high, low], 0)
     )
@@ -511,7 +511,7 @@
     unpack = jnp.concatenate(
         [jnp.where(wide == slots[:, :1] + float(c), 1.0, 0.0).astype(BF16) for c in range(3)], 0
     )
-    own_velocity[...] = dot(unpack, high) + dot(unpack, low)
+    own_velocity[0 : 3 * blocks, :] = dot(unpack, high) + dot(unpack, low)
     for b in range(blocks):
         lanes = slice(b * 128, (b + 1) * 128)
         moved[:, lanes] = (
@@ -563,11 +563,11 @@
             pltpu.VMEM((2, 2, 5, 8, 128), F32),
             pltpu.VMEM((2, 2, 5, 8, 128), F32),
             pltpu.VMEM((2, 2, 8, 128), F32),
-            pltpu.VMEM((4 * blocks, 128), F32),
+            pltpu.VMEM((9 * blocks, 128), F32),
             pltpu.VMEM((group * 8, 128), F32),
-            pltpu.VMEM((group * 8, 128), F32),
+            pltpu.VMEM((group * 8 + 8, 128), F32),
             pltpu.VMEM((group, 128, 256), BF16),
-            pltpu.VMEM((chips // 2 * 192, 128), F32),
+            pltpu.VMEM((chips // 2 * 192 + 8, 128), F32),
             pltpu.VMEM((chips, 2, 8, 128), F32),
             pltpu.VMEM((3, 8, 8, 128), F32),
             pltpu.VMEM((2, 192, 128), BF16),
@@ -591,7 +591,7 @@
         in_specs=[in_vmem] * 4,
         out_specs=(in_hbm, in_hbm),
         scratch_shapes=[
-            pltpu.VMEM((3 * blocks, 128), F32),
+            pltpu.VMEM((9 * blocks, 128), F32),
             pltpu.VMEM(tracer_ref.shape, F32),
             pltpu.SemaphoreType.DMA((2,)),
         ],

time: 18.8 us -> 18.8 us (level)
  no operation moved by 1% of the time
where the time goes in v7:
time: 18.8 us; the launch traced here: 18.7 us
  Pallas kernels  18.1 us (96%)
  between operations  0.64 us (3%)
    pallas_call x1, Pallas kernels, shards(): pl.pallas_call(functools.partial(body, (n_gx, n_gy, n_gz, blocks)), out_s...  17.2 us
    pallas_call x1, Pallas kernels, shards(): pl.pallas_call(finish, out_shape=(jax.ShapeDtypeStruct(fields.shape, F32)...  0.9 us

profile of v7, /device:TPU:64, one launch (start us, length us, event | category | flops | bytes accessed | tf_op | source)
XLA Modules:
  0.0 18.7 jit_solution(18403281246888389237)
XLA Ops:
  0.6 17.2 %shard_map.77 = (f32[5,8,8,128]{3,2,1,0:T(8,128)S(1)}, f32[16,2,8,128]{3,2,1,0:T(8,128)S(1)}, f32[3,4096]{1,0:T(4,128)S(1)}, f32[32,128]{1,0:T(8,128)S(1)}) custom-call(f32[5,8,8,128]{3,2,1,0:T(8,128)} %fields_hbm.1, f32[3,4096]{1,0:T(4,128)} %tracer_hbm.1, s32[32,128]{1,0:T(8,128)} %bitcast.2, s32[1,32]{1,0:T(1,128)} %bitcast.3, ...), custom_call_target="tpu_custom_call" | custom-call | tf_op jit(solution)/shard_map/pallas_call | solution.py:541
  17.8 0.9 %shard_map.78 = (f32[5,8,8,128]{3,2,1,0:T(8,128)}, f32[3,4096]{1,0:T(4,128)}) custom-call(f32[5,8,8,128]{3,2,1,0:T(8,128)S(1)} %get-tuple-element.6.final, f32[16,2,8,128]{3,2,1,0:T(8,128)S(1)} %get-tuple-element.7.returned, f32[3,4096]{1,0:T(4,128)S(1)} %get-tuple-element.8.tracer, f32[32,128]{1,0:T(8,128)S(1)} %get-tuple-element.9.slots), custom_call_target="tpu_custom_call" | custom-call | tf_op jit(solution)/shard_map/pallas_call | solution.py:585
